TPU v7x, 256 devices: a whole 4x4x8 slice. The times are simulated.
256 devices in a mesh: dp: 8 (over y, core), ctx: 32 (over z, x).
Axes of the slice: x: 4, y: 4, z: 8, core: 2. Of those that a mesh axis runs over, the one named last changes fastest.
Arguments:
- queries: bfloat16 [32768, 4096], P(('dp', 'ctx')), may hold values from -6.25 to 6.25
- keys: bfloat16 [32768, 512], P(('dp', 'ctx')), may hold values from -6.25 to 6.25
- values: bfloat16 [32768, 512], P(('dp', 'ctx')), may hold values from -6 to 6
- grad_out: bfloat16 [32768, 4096], P(('dp', 'ctx')), may hold values from -6 to 6
- inputs: bfloat16 [32768, 3072], P(('dp', 'ctx')), may hold values from -0.125 to 0.125
- span_map: int32 [8, 64], P('dp'), may hold values from 0 to 63, each once within a row
- doc_lengths: int32 [8, 32], P('dp'), may hold values from 1 to 256, 4096 in all within a row
Outputs:
- query_grads: bfloat16 [32768, 4096], P(('dp', 'ctx'))
- weight_grads: float32 [3072, 1024], P(('dp', 'ctx'))
Inputs may be any that keep to these rules, and one draw needn't show every extreme that they name: `span_map`: each row lists every span of its sequence exactly once. `doc_lengths`: each row holds the lengths of consecutive documents that fill its sequence of 4096 tokens exactly, and its longest document has 256 tokens.
All inputs are finite; a program needn't handle non-finite values.
Results may differ from a plain program's by a relative error of at most 0.02.
Values may be sent and summed in bfloat16 or wider, within the bound.
A program may use at most 128 MiB of HBM per device.

v0:
```python
import jax
import jax.numpy as jnp
from jax import lax
from jax.sharding import PartitionSpec as P

H = 32
KVH = 4
HD = 128
ROT = 64


ROPE_BASE = 10000000.0
MASKED_SCORE = -1e30


def table_pick(lookup_table, lookup_index):
    table_spots = jnp.arange(lookup_table.shape[0], dtype=jnp.int32)
    picked = jnp.where(lookup_index[:, None] == table_spots[None, :], lookup_table[None, :], 0)
    return jnp.sum(picked, axis=1)


def doc_begin(positions, lengths):
    doc_ends = jnp.cumsum(lengths)
    starts = doc_ends - lengths
    picked = jnp.where(starts[None, :] <= positions[:, None], starts[None, :], 0)
    return jnp.max(picked, axis=1)


def rotary(vectors, relative, direction_sign):
    half_rot = ROT // 2
    frequency = ROPE_BASE ** (-(jnp.arange(half_rot, dtype=jnp.float32) * 2.0 / ROT))
    angles = relative.astype(jnp.float32)[:, None] * frequency[None, :]
    cosine = jnp.cos(angles)[:, None, :]
    sine_part = direction_sign * jnp.sin(angles)[:, None, :]
    first_half = vectors[..., :half_rot]
    second = vectors[..., half_rot:ROT]
    return jnp.concatenate(
        [
            first_half * cosine - second * sine_part,
            second * cosine + first_half * sine_part,
            vectors[..., ROT:],
        ],
        axis=-1,
    )


def window_grads(packed):
    query_rot, dout, key_window, value_window, allowed = packed
    scaling = HD ** (-0.5)
    mask_full = allowed[None, None, :, :]
    scores = (
        jnp.einsum("qjgd,kjd->jgqk", query_rot, key_window, preferred_element_type=jnp.float32)
        * scaling
    )
    row_top = jnp.max(jnp.where(mask_full, scores, MASKED_SCORE), axis=-1, keepdims=True)
    row_total = jnp.sum(
        jnp.where(mask_full, jnp.exp(scores - row_top), 0.0), axis=-1, keepdims=True
    )
    log_total = row_top + jnp.log(row_total)
    probability = jnp.where(mask_full, jnp.exp(scores - log_total), 0.0)
    dprobs = jnp.einsum("qjgd,kjd->jgqk", dout, value_window, preferred_element_type=jnp.float32)
    delta_row = jnp.sum(probability * dprobs, axis=-1, keepdims=True)
    dscores = (probability * (dprobs - delta_row)).astype(jnp.bfloat16)
    probs_low = probability.astype(jnp.bfloat16)
    query_part = (
        jnp.einsum("jgqk,kjd->qjgd", dscores, key_window, preferred_element_type=jnp.float32)
        * scaling
    )
    key_part = (
        jnp.einsum("jgqk,qjgd->kjd", dscores, query_rot, preferred_element_type=jnp.float32)
        * scaling
    )
    value_part = jnp.einsum("jgqk,qjgd->kjd", probs_low, dout, preferred_element_type=jnp.float32)
    return (query_part, key_part, value_part)


def per_device(queries, keys, values, grad_out, inputs, span_map, doc_lengths):
    rows_dev = queries.shape[0]
    half_rows = rows_dev // 2
    count_ctx = lax.axis_size("ctx")
    slot_count = 2 * count_ctx
    seq_rows = slot_count * half_rows
    longest = min(2 * rows_dev, seq_rows // 2)
    reach_back = longest // half_rows
    window_len = reach_back + 1
    groups = H // KVH
    kv_cols = KVH * HD
    span_order = span_map[0]
    lengths = doc_lengths[0]
    my_index = lax.axis_index("ctx")
    local_rows = jnp.arange(rows_dev, dtype=jnp.int32)
    my_slots = 2 * my_index + jnp.arange(2, dtype=jnp.int32)
    my_spans = table_pick(span_order, my_slots)
    positions = jnp.repeat(my_spans, half_rows) * half_rows + local_rows % half_rows
    begins = doc_begin(positions, lengths)
    relative = positions - begins
    query_rot = rotary(queries.reshape(rows_dev, H, HD).astype(jnp.float32), relative, 1.0).astype(
        jnp.bfloat16
    )
    key_rot = rotary(keys.reshape(rows_dev, KVH, HD).astype(jnp.float32), relative, 1.0).astype(
        jnp.bfloat16
    )
    key_rot = key_rot.reshape(rows_dev, kv_cols)
    span_ids = jnp.arange(slot_count, dtype=jnp.int32)
    slot_of = jnp.sum(
        jnp.where(span_order[None, :] == span_ids[:, None], span_ids[None, :], 0), axis=1
    )
    steps_back = jnp.arange(window_len, dtype=jnp.int32) - reach_back
    win_spans = my_spans[:, None] + steps_back[None, :]
    live_span = win_spans >= 0
    win_spans = jnp.maximum(win_spans, 0)
    win_slots = table_pick(slot_of, win_spans.reshape(-1)).reshape(2, window_len)
    key_all, value_all = (
        lax.all_gather(key_rot, "ctx", axis=0, tiled=True),
        lax.all_gather(values, "ctx", axis=0, tiled=True),
    )
    key_spans = key_all.reshape(slot_count, half_rows, kv_cols)[win_slots]
    value_spans = value_all.reshape(slot_count, half_rows, kv_cols)[win_slots]
    key_window = key_spans.reshape(2, window_len * half_rows, KVH, HD)
    value_window = value_spans.reshape(2, window_len * half_rows, KVH, HD)
    span_rows = jnp.arange(half_rows, dtype=jnp.int32)
    key_pos = (win_spans[:, :, None] * half_rows + span_rows[None, None, :]).reshape(2, -1)
    key_live = jnp.repeat(live_span, half_rows, axis=1)
    query_pos = positions.reshape(2, half_rows)
    query_begin = begins.reshape(2, half_rows)
    allowed = (
        key_live[:, None, :]
        & (key_pos[:, None, :] <= query_pos[:, :, None])
        & (key_pos[:, None, :] >= query_begin[:, :, None])
    )
    query_five = query_rot.reshape(2, half_rows, KVH, groups, HD)
    dout_five = grad_out.reshape(2, half_rows, KVH, groups, HD)
    query_part, key_part, value_part = lax.map(
        window_grads, (query_five, dout_five, key_window, value_window, allowed)
    )
    contrib = jnp.concatenate(
        [
            key_part.reshape(2 * window_len, half_rows, kv_cols),
            value_part.reshape(2 * window_len, half_rows, kv_cols),
        ],
        axis=-1,
    )
    flat_slots = win_slots.reshape(-1)
    same_slot = (flat_slots[:, None] == flat_slots[None, :]).astype(jnp.float32)
    merged = jnp.dot(
        same_slot,
        contrib.reshape(2 * window_len, -1),
        precision=lax.Precision.HIGHEST,
        preferred_element_type=jnp.float32,
    )
    partial_value = (
        jnp.zeros((slot_count, half_rows * 2 * kv_cols), jnp.bfloat16)
        .at[flat_slots]
        .set(merged.astype(jnp.bfloat16))
    )
    partial_value = partial_value.reshape(seq_rows, 2 * kv_cols)
    key_grads = lax.psum_scatter(partial_value, "ctx", scatter_dimension=0, tiled=True).astype(
        jnp.float32
    )
    grad_key = rotary(key_grads[:, :kv_cols].reshape(rows_dev, KVH, HD), relative, -1.0).reshape(
        rows_dev, kv_cols
    )
    grads_low = jnp.concatenate([grad_key, key_grads[:, kv_cols:]], axis=1).astype(jnp.bfloat16)
    grad_query = rotary(query_part.reshape(rows_dev, H, HD), relative, -1.0)
    query_grads = grad_query.reshape(rows_dev, H * HD).astype(jnp.bfloat16)
    weight_grads = lax.psum_scatter(
        lax.dot_general(
            inputs, grads_low, (((0,), (0,)), ((), ())), preferred_element_type=jnp.float32
        ),
        ("dp", "ctx"),
        scatter_dimension=0,
        tiled=True,
    )
    return (query_grads, weight_grads)


def solution(mesh):
    in_specs = (
        P(("dp", "ctx"), None),
        P(("dp", "ctx"), None),
        P(("dp", "ctx"), None),
        P(("dp", "ctx"), None),
        P(("dp", "ctx"), None),
        P("dp", None),
        P("dp", None),
    )
    out_specs = (P(("dp", "ctx"), None), P(("dp", "ctx"), None))
    return jax.shard_map(
        per_device, mesh=mesh, in_specs=in_specs, out_specs=out_specs, check_vma=False
    )
```

profile of v0, /device:TPU:1, one launch (start us, length us, event | category | flops | bytes accessed | tf_op | source)
XLA Modules:
  0.0 810.5 jit_solution(14173928668174408257)
XLA Ops:
  7.2 1.1 convert_element_type.45
  8.5 0.8 fusion.38
  9.5 0.9 reduce-window_clone.1
  11.1 0.9 broadcast_multiply_fusion
  16.0 2.2 copy.49
  18.6 0.8 subtract_convert_fusion.1
  19.4 1.0 copy.48
  20.4 1.7 copy.47
  22.2 5.3 pad_maximum_fusion.1
  27.5 4.7 copy.36
  32.2 1.4 copy.63
  34.4 62.1 %all-gather.3.cloned.1.call-done = bf16[4096,512]{1,0:T(8,128)(2,1)} async-done(((bf16[128,512]{1,0:T(8,128)(2,1)}), bf16[4096,512]{1,0:T(8,128)(2,1)}) %all-gather.3.cloned.1.call-update) | async-done | bytes 4194320 | tf_op jit(solution)/shard_map/all_gather | solution.py:114
  96.5 3.6 gather_fusion
  100.2 1.6 reshape.335
  101.8 76.5 %all-gather.5.cloned.1.call-done = bf16[4096,512]{1,0:T(8,128)(2,1)} async-done(((bf16[128,512]{1,0:T(8,128)(2,1)}), bf16[4096,512]{1,0:T(8,128)(2,1)}) %all-gather.5.cloned.1.call-update) | async-done | bytes 4194320 | tf_op jit(solution)/shard_map/all_gather | solution.py:115
  178.3 3.6 gather_fusion.1
  181.9 2.3 reshape.337
  184.3 28.3 %while.14 = (s32[]{:T(128)}, f32[2,64,4,8,128]{4,3,2,1,0:T(8,128)}, f32[2,320,4,128]{3,2,1,0:T(4,128)}, f32[2,320,4,128]{3,2,1,0:T(4,128)}, bf16[2,320,4,128]{3,...) while((s32[]{:T(128)}, f32[2,64,4,8,128]{4,3,2,1,0:T(8,128)}, ...), condition=%wide.region_9.10_spmd, body=%wide.region_5.9_spmd.sunk | while | flops 853700608 | bytes 75669840 | solution.py:133
  186.1 1.1 fusion.65
  187.4 1.3 fusion.66
  188.7 2.0 fusion.67
  191.3 1.0 copy-done.1
  193.0 1.3 fusion.69
  196.1 0.9 copy_dynamic-update-slice_fusion.6
  197.1 1.0 copy-done.9
  200.2 1.1 fusion.65
  201.5 1.3 fusion.66
  202.7 2.0 fusion.67
  205.3 1.0 copy-done.1
  207.0 1.3 fusion.69
  210.1 0.9 copy_dynamic-update-slice_fusion.6
  211.1 1.0 copy-done.9
  212.6 1.8 reshape.341
  214.4 2.3 reshape.340
  217.5 2.4 copy.65
  219.9 2.2 convolution_convert_fusion
  222.1 3.8 broadcast_in_dim.142
  225.9 43.4 %scatter_fusion = bf16[64,65536]{1,0:T(8,128)(2,1)} fusion(bf16[64,65536]{1,0:T(8,128)(2,1)} %broadcast_in_dim.142, s32[10]{0:T(128)S(1)} %fusion.42, bf16[10,65536]{1,0:T(8,128)(2,1)S(1)} %convolution_convert_fusion), kind=kCustom, calls=%fused_computation.2 | custom fusion | bytes 3932200 | tf_op jit(solution)/shard_map/scatter | solution.py:154
  269.3 10.6 %reshape.343 = bf16[4096,1024]{1,0:T(8,128)(2,1)} reshape(bf16[64,65536]{1,0:T(8,128)(2,1)} %scatter_fusion) | data formatting | bytes 16777216 | tf_op jit(solution)/shard_map/reshape | solution.py:156
  280.0 224.7 %reduce-scatter.3.cloned.1.call-done = bf16[128,1024]{1,0:T(8,128)(2,1)} async-done(((bf16[4096,1024]{1,0:T(8,128)(2,1)}), bf16[128,1024]{1,0:T(8,128)(2,1)}) %reduce-scatter.3.cloned.1.call-update) | async-done | bytes 262160 | tf_op jit(solution)/shard_map/reduce_scatter | solution.py:157
  504.7 1.0 fusion.44
  506.5 6.3 convolution_bitcast_fusion.1
  512.9 1.6 copy-done.3
  515.6 1.0 pad_maximum_fusion.2
  516.5 1.4 copy.87
  518.0 283.5 %all-reduce.3.cloned.1.call-done = f32[3072,1024]{0,1:T(8,128)} async-done(((f32[3072,1024]{0,1:T(8,128)}), f32[3072,1024]{0,1:T(8,128)}) %all-reduce.3.cloned.1.call-update) | async-done | bytes 12582928
  801.5 1.4 constant_dynamic-slice_fusion.3
  802.9 0.8 copy.42
  (116 shorter events, 19.3 us)
Async XLA Ops:
  7.2 499.4 %copy-start = (bf16[128,3072]{1,0:T(8,128)(2,1)S(1)}, bf16[128,3072]{1,0:T(8,128)(2,1)}, u32[]{:S(2)}) copy-start(bf16[128,3072]{1,0:T(8,128)(2,1)} %param.13) | copy-start | bytes 2359300
  7.2 7.3 copy-start.14
  7.2 8.2 %copy-start.12 = (bf16[128,4096]{1,0:T(8,128)(2,1)S(1)}, bf16[128,4096]{1,0:T(8,128)(2,1)}, u32[]{:S(2)}) copy-start(bf16[128,4096]{1,0:T(8,128)(2,1)} %param.9) | copy-start | bytes 3145732
  7.2 89.3 %all-gather.3.cloned.1.call-start = ((), (), s32[]{:S(2)}) async-start(), calls=%async_computation.1 | async-start | bytes 4325376 | tf_op jit(solution)/shard_map/all_gather | solution.py:114
  12.1 6.5 copy-start.6
  13.4 164.9 %all-gather.5.cloned.1.call-start = ((), (), s32[]{:S(2)}) async-start(), calls=%async_computation.2 | async-start | bytes 4325376 | tf_op jit(solution)/shard_map/all_gather | solution.py:115
  14.1 490.5 %reduce-scatter.3.cloned.1.call-start = ((), (), s32[]{:S(2)}) async-start(), calls=%async_computation.3 | async-start | bytes 8650752 | tf_op jit(solution)/shard_map/reduce_scatter | solution.py:157
  20.4 1.7 copy-start.5
  186.1 1.1 copy-start.4
  190.7 1.6 copy-start.1
  193.0 1.4 copy-start.2
  194.4 1.3 copy-start.8
  194.4 1.7 copy-start.10
  197.0 1.1 copy-start.9
  197.0 1.5 copy-start.11
  200.2 1.1 copy-start.4
  204.7 1.6 copy-start.1
  207.0 1.4 copy-start.2
  208.4 1.3 copy-start.8
  208.4 1.7 copy-start.10
  211.1 1.1 copy-start.9
  211.1 1.5 copy-start.11
  279.9 226.0 %copy-start.7 = (f32[128,32]{1,0:T(8,128)S(1)}, f32[128,32]{1,0:T(8,128)}, u32[]{:S(2)}) copy-start(f32[128,32]{1,0:T(8,128)} %copy-done.6) | copy-start | bytes 49156
  279.9 226.0 %copy-start.13 = (f32[128,32]{1,0:T(8,128)S(1)}, f32[128,32]{1,0:T(8,128)}, u32[]{:S(2)}) copy-start(f32[128,32]{1,0:T(8,128)} %get-tuple-element.123) | copy-start | bytes 49156
  279.9 521.5 %all-reduce.3.cloned.1.call-start = ((), (), s32[]{:S(2)}) async-start(), calls=%async_computation.4 | async-start | bytes 25165824
  512.8 1.6 copy-start.3
Sparse Core Ops, SparseCore 0:
  13.5 82.9 all-gather.2
  99.1 79.1 all-gather.4
  280.0 224.5 reduce-scatter.2
  513.0 288.4 all-reduce.2
where the time goes:
time: 818 us; the launch traced here: 810 us
  waiting for transfers between devices  647 us (79%)
  local copies, waits for them, and re-layouts  110 us (13%)
  other arithmetic  20.5 us (3%)
  matrix products  17.7 us (2%)
  between operations  14.3 us (2%)
    unnamed x5, waiting for transfers between devices  284 us
    reduce_scatter x1, waiting for transfers between devices, per_device(): lax.psum_scatter(partial_value, 'ctx', scatter_dimension=0, tiled=True)  225 us
    all_gather x1, waiting for transfers between devices, per_device(): lax.all_gather(values, 'ctx', axis=0, tiled=True)  76.5 us
    all_gather x1, waiting for transfers between devices, per_device(): lax.all_gather(key_rot, 'ctx', axis=0, tiled=True)  62.1 us
    scatter x1, local copies, waits for them, and re-layouts, per_device(): partial_value = jnp.zeros((slot_count, half_rows * 2 * kv_cols), jnp.bflo...  43.4 us
  transfers between devices with their start and end apart: 4, of which 4 were waited for; matrix products, arithmetic and copies ran while one was open for 4% of the time, Pallas kernels for 0%

commit v1 on v0

v1 whole, which is shorter than its diff:
```python
import functools

import jax
import jax.numpy as jnp
import numpy as np
from jax import lax
from jax.experimental import pallas as pl
from jax.experimental.pallas import tpu as pltpu
from jax.sharding import PartitionSpec as P

MESH = pl.DeviceIdType.MESH
BF16 = jnp.bfloat16
F32 = jnp.float32

KVH = 4
G = 8
HD = 128
ROT = 64
ROPE_BASE = 10000000.0
SPAN = 64
BACK = 4
ROWS = 2 * SPAN
N_CTX = 32
N_DP = 8
N_X = 4
N_Z = 8
SLOTS = 2 * N_CTX
NDOC = 32
KVC = KVH * HD
PIECE = 16
REACH = 2 * BACK
W_DP = 384
W_DEV = W_DP // N_CTX
W_X = W_DP // N_X
MASKED = -1e30
VMEM_LIMIT = 48 * 1024 * 1024

NT = (((1,), (1,)), ((), ()))
TN = (((0,), (0,)), ((), ()))


def rope_lanes():
    half = ROT // 2
    freq = ROPE_BASE ** (-(np.arange(half, dtype=np.float64) * 2.0 / ROT))
    row = np.zeros((1, HD), np.float32)
    row[0, :half] = freq
    row[0, half:ROT] = freq
    return row


def feature_order():
    order = np.arange(W_DP).reshape(N_Z, N_X, W_DEV).transpose(1, 0, 2).reshape(-1)
    return np.eye(W_DP, dtype=np.float32)[order]


def swap_halves(x):
    lane = lax.broadcasted_iota(jnp.int32, x.shape, 1)
    return jnp.where(lane < ROT // 2, pltpu.roll(x, HD - ROT // 2, 1), pltpu.roll(x, ROT // 2, 1))


def begin_of(pos, len_ref):
    def step(d, carry):
        start, begin = carry
        return start + len_ref[0, d], jnp.where(pos >= start, start, begin)

    _, begin = lax.fori_loop(0, NDOC, step, (jnp.int32(0), jnp.zeros_like(pos)), unroll=True)
    return begin


def prep_kernel(span_ref, len_ref, freq_ref, key_ref, val_ref, pack_ref, cos_ref, sin_ref, slot_ref):
    me = lax.axis_index("ctx")

    def place(slot, carry):
        slot_ref[0, span_ref[0, slot]] = slot
        return carry

    lax.fori_loop(0, SLOTS, place, 0, unroll=8)
    row = lax.broadcasted_iota(jnp.int32, (ROWS, HD), 0)
    lane = lax.broadcasted_iota(jnp.int32, (ROWS, HD), 1)
    second = row >= SPAN
    span = jnp.where(second, span_ref[0, 2 * me + 1], span_ref[0, 2 * me])
    pos = span * SPAN + jnp.where(second, row - SPAN, row)
    rel = (pos - begin_of(pos, len_ref)).astype(F32)
    angle = rel * freq_ref[...]
    sine = jnp.sin(angle)
    cos = jnp.where(lane < ROT, jnp.cos(angle), 1.0)
    sin = jnp.where(lane < ROT // 2, -sine, jnp.where(lane < ROT, sine, 0.0))
    cos_ref[...] = cos
    sin_ref[...] = sin
    for j in range(KVH):
        k = key_ref[:, j * HD : (j + 1) * HD].astype(F32)
        k = (k * cos + swap_halves(k) * sin).astype(BF16)
        v = val_ref[:, j * HD : (j + 1) * HD]
        for s in range(2):
            for r in range(SPAN // PIECE):
                at = s * SPAN + r * PIECE
                pack_ref[r * KVH + j, s] = k[at : at + PIECE]
                pack_ref[16 + r * KVH + j, s] = v[at : at + PIECE]


def greet(peers):
    barrier = pltpu.get_barrier_semaphore()
    count = 0
    for first, last, device in peers:

        def hello(k, carry, device=device):
            pl.semaphore_signal(barrier, inc=1, device_id=device(k), device_id_type=MESH)
            return carry

        lax.fori_loop(first, last, hello, 0)
        count += last - first
    pl.semaphore_wait(barrier, count)


def loop(first, last, body):
    def step(k, carry):
        body(k)
        return carry

    lax.fori_loop(first, last, step, 0)


def remote(src, dst, send, recv, device):
    return pltpu.make_async_remote_copy(
        src_ref=src, dst_ref=dst, send_sem=send, recv_sem=recv, device_id=device, device_id_type=MESH
    )


def gather_kernel(
    span_ref, slot_ref, pack_ref, inputs_ref, win_ref, x_ref,
    held, chosen, take, send1, recv1, send2, recv2, send3, recv3, own_sem,
):
    dp, me = lax.axis_index("dp"), lax.axis_index("ctx")
    ctx_peer = lambda k: lax.rem(me + k, N_CTX)
    dp_peer = lambda k: lax.rem(dp + k, N_DP)
    greet([(1, N_CTX, lambda k: (dp, ctx_peer(k))), (1, N_DP, lambda k: (dp_peer(k), me))])

    def first_copy(src, owner, peer):
        return remote(
            pack_ref.at[src], held.at[pl.ds(2 * owner, 2)], send1.at[src], recv1.at[owner], (dp, peer)
        )

    def input_copy(part, owner, peer):
        cols = pl.ds(pl.multiple_of(part * W_DP, W_DP), W_DP)
        return remote(inputs_ref.at[:, cols], x_ref.at[owner], send3.at[part], recv3.at[owner], (peer, me))

    def second_copy(src, owner, peer):
        return remote(chosen.at[src], win_ref.at[owner], send2.at[src], recv2.at[owner], (dp, peer))

    loop(1, N_CTX, lambda k: first_copy(ctx_peer(k), me, ctx_peer(k)).start())
    loop(1, N_DP, lambda k: input_copy(dp_peer(k), dp, dp_peer(k)).start())
    own_cols = pl.ds(pl.multiple_of(dp * W_DP, W_DP), W_DP)
    own_copy = pltpu.make_async_copy(inputs_ref.at[:, own_cols], x_ref.at[dp], own_sem)
    own_copy.start()
    held[pl.ds(2 * me, 2)] = pack_ref[me]

    def fill(slot):
        span = span_ref[0, slot]
        for w in range(BACK):
            take[slot * BACK + w] = slot_ref[0, jnp.maximum(span - BACK + w, 0)]

    loop(0, SLOTS, fill)
    loop(1, N_CTX, lambda k: first_copy(me, ctx_peer(k), ctx_peer(k)).wait_recv())

    def choose(j):
        for w in range(REACH):
            chosen[j, w] = held[take[j * REACH + w]]

    def serve(k):
        choose(ctx_peer(k))
        second_copy(ctx_peer(k), me, ctx_peer(k)).start()

    loop(1, N_CTX, serve)
    choose(me)
    win_ref[me] = chosen[me]
    loop(1, N_CTX, lambda k: first_copy(ctx_peer(k), me, ctx_peer(k)).wait_send())
    loop(1, N_DP, lambda k: input_copy(dp_peer(k), dp, dp_peer(k)).wait_send())
    own_copy.wait()
    loop(1, N_DP, lambda k: input_copy(dp, dp_peer(k), dp_peer(k)).wait_recv())
    loop(1, N_CTX, lambda k: second_copy(ctx_peer(k), me, ctx_peer(k)).wait_send())
    loop(1, N_CTX, lambda k: second_copy(me, ctx_peer(k), ctx_peer(k)).wait_recv())


def attend_kernel(
    span_ref, len_ref, q_ref, do_ref, win_ref, pack_ref, cos_ref, sin_ref,
    dq_ref, part_ref, own_ref, bias,
):
    me = lax.axis_index("ctx")
    keys_n = (BACK + 1) * SPAN

    @pl.when(pl.program_id(0) == 0)
    def _():
        for s in range(2):
            span = span_ref[0, 2 * me + s]
            lane = lax.broadcasted_iota(jnp.int32, (8, HD), 1)
            qpos = span * SPAN + jnp.where(lane >= SPAN, lane - SPAN, lane)
            qbegin = begin_of(qpos, len_ref)
            k = lax.broadcasted_iota(jnp.int32, (keys_n, HD), 0)
            r, w, t = k >> 6, (k >> 4) & 3, k & 15
            earlier = (span - BACK + w) * SPAN + r * PIECE + t
            kpos = jnp.where(k < BACK * SPAN, earlier, span * SPAN + (k - BACK * SPAN))
            allowed = (kpos <= qpos[0:1]) & (kpos >= qbegin[0:1])
            bias[s] = jnp.where(allowed, 0.0, MASKED)

    scale = HD**-0.5
    for s in range(2):
        rows = slice(s * SPAN, (s + 1) * SPAN)
        cos, sin = cos_ref[rows], sin_ref[rows]

        def window(kind):
            earlier = win_ref[kind, :, 0, s * BACK : (s + 1) * BACK].reshape(BACK * SPAN, HD)
            mine = pack_ref[kind, :, 0, s].reshape(SPAN, HD)
            return jnp.concatenate([earlier, mine], axis=0)

        def rotated(g):
            x = q_ref[rows, g * HD : (g + 1) * HD].astype(F32)
            return (x * cos + swap_halves(x) * sin).astype(BF16)

        k, v = window(0), window(1)
        q = jnp.concatenate([rotated(g) for g in range(G)], axis=0)
        do = jnp.concatenate([do_ref[rows, g * HD : (g + 1) * HD] for g in range(G)], axis=0)
        mask = jnp.concatenate([bias[s]] * (G * SPAN // HD), axis=1)
        scores = lax.dot_general(k, q, NT, preferred_element_type=F32)
        scores = scores * (scale * float(np.log2(np.e))) + mask
        weight = jnp.exp2(scores - jnp.max(scores, axis=0, keepdims=True))
        probs = weight * (1.0 / jnp.sum(weight, axis=0, keepdims=True))
        dprobs = lax.dot_general(v, do, NT, preferred_element_type=F32)
        delta = jnp.sum(probs * dprobs, axis=0, keepdims=True)
        dscores = (probs * (dprobs - delta)).astype(BF16)
        low = probs.astype(BF16)
        dk = jnp.dot(dscores, q, preferred_element_type=F32) * scale
        dv = jnp.dot(low, do, preferred_element_type=F32)
        dq = lax.dot_general(k, dscores, TN, preferred_element_type=F32).T * scale
        for kind, grad in ((0, dk), (1, dv)):
            earlier = grad[: BACK * SPAN].astype(BF16).reshape(SPAN // PIECE, BACK, PIECE, HD)
            part_ref[kind, :, 0, s * BACK : (s + 1) * BACK] = earlier
            own_ref[kind, rows] = grad[BACK * SPAN :]
        for g in range(G):
            x = dq[g * SPAN : (g + 1) * SPAN]
            dq_ref[rows, g * HD : (g + 1) * HD] = (x * cos - swap_halves(x) * sin).astype(BF16)


def reduce_kernel(
    span_ref, slot_ref, part_ref, own_ref, cos_ref, sin_ref, x_ref, perm_ref, out_ref,
    landed, give, total, back, grads, xt, wsend, xland, zsend, zland,
    send1, recv1, send2, recv2, send3, recv3, send4, recv4, send5, recv5, send6, recv6,
):
    dp, me = lax.axis_index("dp"), lax.axis_index("ctx")
    z, x = me // N_X, lax.rem(me, N_X)
    sib = dp + 1 - 2 * lax.rem(dp, 2)
    ctx_peer = lambda k: lax.rem(me + k, N_CTX)
    y_peer = lambda k: lax.rem(dp + 2 * k, N_DP)
    sib_peer = lambda k: lax.rem(sib + 2 * k, N_DP)
    x_peer = lambda k: lax.rem(x + k, N_X)
    z_peer = lambda k: lax.rem(z + k, N_Z)
    greet([
        (1, N_CTX, lambda k: (dp, ctx_peer(k))),
        (1, 4, lambda k: (y_peer(k), me)),
        (0, 1, lambda k: (sib, me)),
    ])

    def first_copy(src, owner, peer):
        return remote(
            part_ref.at[src], landed.at[pl.ds(REACH * owner, REACH)], send1.at[src], recv1.at[owner], (dp, peer)
        )

    def second_copy(src, owner, peer):
        return remote(total.at[src], back.at[owner], send2.at[src], recv2.at[owner], (dp, peer))

    def y_copy(owner, peer):
        return remote(grads.at[owner], grads.at[owner], send3.at[peer], recv3.at[owner], (peer, me))

    def sib_copy(owner):
        return remote(grads.at[owner], grads.at[owner], send4.at[owner], recv4.at[owner], (sib, me))

    def x_copy(src, owner, peer):
        return remote(wsend.at[src], xland.at[owner], send5.at[src], recv5.at[owner], (dp, z * N_X + peer))

    def z_copy(src, owner, peer):
        return remote(zsend.at[src], zland.at[owner], send6.at[src], recv6.at[owner], (dp, peer * N_X + x))

    loop(1, N_CTX, lambda k: first_copy(ctx_peer(k), me, ctx_peer(k)).start())
    landed[pl.ds(REACH * me, REACH)] = part_ref[me]
    landed[N_CTX * REACH] = jnp.zeros((PIECE, HD), BF16)

    def fill(slot):
        span = span_ref[0, slot]
        for w in range(BACK):
            later = span + 1 + w
            source = slot_ref[0, jnp.minimum(later, SLOTS - 1)] * BACK + (BACK - 1 - w)
            give[slot * BACK + w] = jnp.where(later < SLOTS, source, N_CTX * REACH)

    loop(0, SLOTS, fill)
    for d in range(N_DP):
        turned = lax.dot_general(perm_ref[...], x_ref[d], NT, preferred_element_type=F32)
        xt[:, d * ROWS : (d + 1) * ROWS] = turned.astype(BF16)
    loop(1, N_CTX, lambda k: first_copy(me, ctx_peer(k), ctx_peer(k)).wait_recv())

    def sum_up(j):
        for s in range(2):
            at = (2 * j + s) * BACK
            acc = landed[give[at]].astype(F32)
            for w in range(1, BACK):
                acc += landed[give[at + w]].astype(F32)
            total[j, s] = acc.astype(BF16)

    def serve(k):
        sum_up(ctx_peer(k))
        second_copy(ctx_peer(k), me, ctx_peer(k)).start()

    loop(1, N_CTX, serve)
    sum_up(me)
    back[me] = total[me]
    loop(1, N_CTX, lambda k: first_copy(ctx_peer(k), me, ctx_peer(k)).wait_send())
    loop(1, N_CTX, lambda k: second_copy(me, ctx_peer(k), ctx_peer(k)).wait_recv())
    for kind in range(2):
        for r in range(SPAN // PIECE):
            for j in range(KVH):
                for s in range(2):
                    rows = slice(s * SPAN + r * PIECE, s * SPAN + (r + 1) * PIECE)
                    cols = slice(j * HD, (j + 1) * HD)
                    g = back[kind * 16 + r * KVH + j, s].astype(F32) + own_ref[kind, rows, cols]
                    if kind == 0:
                        g = g * cos_ref[rows] - swap_halves(g) * sin_ref[rows]
                    grads[dp, rows, kind * KVC + j * HD : kind * KVC + (j + 1) * HD] = g.astype(BF16)
    loop(1, 4, lambda k: y_copy(dp, y_peer(k)).start())
    sib_copy(dp).start()
    for k in range(1, 4):
        y_copy(y_peer(k), y_peer(k)).wait_recv()
        sib_copy(y_peer(k)).start()
    loop(1, N_CTX, lambda k: second_copy(ctx_peer(k), me, ctx_peer(k)).wait_send())
    loop(0, 4, lambda k: sib_copy(sib_peer(k)).wait_recv())
    for n in range(4):
        cols = slice(n * 256, (n + 1) * 256)
        acc = jnp.dot(xt[:, :256], grads[0:2, :, cols].reshape(256, 256), preferred_element_type=F32)
        for d in range(1, 4):
            acc += jnp.dot(
                xt[:, d * 256 : (d + 1) * 256],
                grads[2 * d : 2 * d + 2, :, cols].reshape(256, 256),
                preferred_element_type=F32,
            )
        wsend[:, :, cols] = acc.astype(BF16).reshape(N_X, W_X, 256)
    loop(1, N_X, lambda k: x_copy(x_peer(k), x, x_peer(k)).start())
    loop(1, 4, lambda k: y_copy(dp, y_peer(k)).wait_send())
    loop(0, 4, lambda k: sib_copy(y_peer(k)).wait_send())
    xland[x] = wsend[x]
    loop(1, N_X, lambda k: x_copy(x, x_peer(k), x_peer(k)).wait_recv())
    acc = xland[0].astype(F32)
    for n in range(1, N_X):
        acc += xland[n].astype(F32)
    pad = jnp.zeros((PIECE - W_DEV, 2 * KVC), F32)
    for n in range(N_Z):
        block = jnp.concatenate([acc[n * W_DEV : (n + 1) * W_DEV], pad], axis=0)
        zsend[n] = block.astype(BF16)
    loop(1, N_Z, lambda k: z_copy(z_peer(k), z, z_peer(k)).start())
    zland[z] = zsend[z]
    loop(1, N_X, lambda k: x_copy(x_peer(k), x, x_peer(k)).wait_send())
    loop(1, N_Z, lambda k: z_copy(z, z_peer(k), z_peer(k)).wait_recv())
    acc = zland[0].astype(F32)
    for n in range(1, N_Z):
        acc += zland[n].astype(F32)
    out_ref[...] = acc[:W_DEV]
    loop(1, N_Z, lambda k: z_copy(z_peer(k), z, z_peer(k)).wait_send())


def per_device(queries, keys, values, grad_out, inputs, span_map, doc_lengths):
    smem = pl.BlockSpec(memory_space=pltpu.SMEM)
    vmem = pl.BlockSpec(memory_space=pltpu.VMEM)
    hbm = pl.BlockSpec(memory_space=pl.ANY)
    dma = pltpu.SemaphoreType.DMA
    params = functools.partial(pltpu.CompilerParams, vmem_limit_bytes=VMEM_LIMIT)
    shape = jax.ShapeDtypeStruct

    pack, cos, sin, slot_of = pl.pallas_call(
        prep_kernel,
        out_shape=[
            shape((N_CTX, 2, PIECE, HD), BF16),
            shape((ROWS, HD), F32),
            shape((ROWS, HD), F32),
            shape((1, SLOTS), jnp.int32),
        ],
        in_specs=[smem, smem, vmem, vmem, vmem],
        out_specs=[vmem, vmem, vmem, smem],
        compiler_params=params(),
        name="prep",
    )(span_map, doc_lengths, jnp.asarray(rope_lanes()), keys, values)

    win, x = pl.pallas_call(
        gather_kernel,
        out_shape=[
            shape((N_CTX, REACH, PIECE, HD), BF16),
            shape((N_DP, ROWS, W_DP), BF16),
        ],
        in_specs=[smem, smem, vmem, hbm],
        out_specs=[vmem, vmem],
        scratch_shapes=[
            pltpu.VMEM((SLOTS, PIECE, HD), BF16),
            pltpu.VMEM((N_CTX, REACH, PIECE, HD), BF16),
            pltpu.SMEM((SLOTS * BACK,), jnp.int32),
            dma((N_CTX,)), dma((N_CTX,)),
            dma((N_CTX,)), dma((N_CTX,)),
            dma((N_DP,)), dma((N_DP,)),
            dma,
        ],
        compiler_params=params(collective_id=0, has_side_effects=True),
        name="gather",
    )(span_map, slot_of, pack, inputs)

    pieces = (2, SPAN // PIECE, KVH)
    block = (2, SPAN // PIECE, 1)
    dq, part, own = pl.pallas_call(
        attend_kernel,
        grid=(KVH,),
        out_shape=[
            shape((ROWS, KVH * G * HD), BF16),
            shape(pieces + (REACH, PIECE, HD), BF16),
            shape((2, ROWS, KVC), F32),
        ],
        in_specs=[
            smem,
            smem,
            pl.BlockSpec((ROWS, G * HD), lambda j: (0, j)),
            pl.BlockSpec((ROWS, G * HD), lambda j: (0, j)),
            pl.BlockSpec(block + (REACH, PIECE, HD), lambda j: (0, 0, j, 0, 0, 0)),
            pl.BlockSpec(block + (2, PIECE, HD), lambda j: (0, 0, j, 0, 0, 0)),
            pl.BlockSpec((ROWS, HD), lambda j: (0, 0)),
            pl.BlockSpec((ROWS, HD), lambda j: (0, 0)),
        ],
        out_specs=[
            pl.BlockSpec((ROWS, G * HD), lambda j: (0, j)),
            pl.BlockSpec(block + (REACH, PIECE, HD), lambda j: (0, 0, j, 0, 0, 0)),
            pl.BlockSpec((2, ROWS, HD), lambda j: (0, 0, j)),
        ],
        scratch_shapes=[pltpu.VMEM((2, (BACK + 1) * SPAN, HD), F32)],
        compiler_params=params(),
        name="attend",
    )(
        span_map, doc_lengths, queries, grad_out,
        win.reshape(pieces + (REACH, PIECE, HD)), pack.reshape(pieces + (2, PIECE, HD)), cos, sin,
    )

    weight = pl.pallas_call(
        reduce_kernel,
        out_shape=shape((W_DEV, 2 * KVC), F32),
        in_specs=[smem, smem, vmem, vmem, vmem, vmem, vmem, vmem],
        out_specs=vmem,
        scratch_shapes=[
            pltpu.VMEM((N_CTX * REACH + 1, PIECE, HD), BF16),
            pltpu.SMEM((SLOTS * BACK,), jnp.int32),
            pltpu.VMEM((N_CTX, 2, PIECE, HD), BF16),
            pltpu.VMEM((N_CTX, 2, PIECE, HD), BF16),
            pltpu.VMEM((N_DP, ROWS, 2 * KVC), BF16),
            pltpu.VMEM((W_DP, N_DP * ROWS), BF16),
            pltpu.VMEM((N_X, W_X, 2 * KVC), BF16),
            pltpu.VMEM((N_X, W_X, 2 * KVC), BF16),
            pltpu.VMEM((N_Z, PIECE, 2 * KVC), BF16),
            pltpu.VMEM((N_Z, PIECE, 2 * KVC), BF16),
            dma((N_CTX,)), dma((N_CTX,)),
            dma((N_CTX,)), dma((N_CTX,)),
            dma((N_DP,)), dma((N_DP,)),
            dma((N_DP,)), dma((N_DP,)),
            dma((N_X,)), dma((N_X,)),
            dma((N_Z,)), dma((N_Z,)),
        ],
        compiler_params=params(collective_id=1, has_side_effects=True),
        name="reduce",
    )(
        span_map, slot_of, part.reshape(N_CTX, REACH, PIECE, HD), own, cos, sin, x,
        jnp.asarray(feature_order(), BF16),
    )
    return dq, weight


def solution(mesh):
    rows = P(("dp", "ctx"), None)
    return jax.shard_map(
        per_device,
        mesh=mesh,
        in_specs=(rows, rows, rows, rows, rows, P("dp", None), P("dp", None)),
        out_specs=(rows, rows),
        check_vma=False,
    )
```

time: 818 us -> 141 us (0.17)
  waiting for transfers between devices: 647 us -> 0 us
  Pallas kernels: 0 us -> 133 us
  local copies, waits for them, and re-layouts: 110 us -> 6.76 us
  other arithmetic: 20.5 us -> 0 us
  matrix products: 17.7 us -> 0 us
  between operations: 14.3 us -> 0.69 us
    unnamed x5 -> x0, waiting for transfers between devices: 284 us -> none
    reduce_scatter x1 -> x0, waiting for transfers between devices: 225 us -> none  [per_device(): lax.psum_scatter(partial_value, 'ctx', scatter_dimension=0, tiled=True)]
    all_gather x2 -> x0, waiting for transfers between devices: 139 us -> none  [the longest x1 76.5 us: per_device(): lax.all_gather(values, 'ctx', axis=0, tiled=True)]
    pallas_call x0 -> x4, Pallas kernels: none -> 133 us  [the longest x1 80 us: per_device(): pl.pallas_call(reduce_kernel, out_shape=shape((W_DEV, 2 * KVC), F32), in_...]
    scatter x1 -> x0, local copies, waits for them, and re-layouts: 43.4 us -> none  [per_device(): partial_value = jnp.zeros((slot_count, half_rows * 2 * kv_cols), jnp.bflo...]
    reshape x7 -> x0, local copies, waits for them, and re-layouts: 18.8 us -> none  [the longest x1 10.6 us: per_device(): partial_value = partial_value.reshape(seq_rows, 2 * kv_cols)]
    dot_general x12 -> x0, matrix products: 17.7 us -> none  [the longest x1 6.3 us: per_device(): lax.dot_general(inputs, grads_low, (((0,), (0,)), ((), ())), preferred_el...]
    while x29 -> x0, local copies, waits for them, and re-layouts: 11.8 us -> none
  transfers between devices with their start and end apart: 4 -> 0, of which waited for: 4 -> 0; matrix products, arithmetic and copies ran while one was open for 4% -> 0% of each run, Pallas kernels for 0% -> 0%
where the time goes in v1:
time: 141 us; the launch traced here: 140 us
  Pallas kernels  133 us (94%)
  local copies, waits for them, and re-layouts  6.76 us (5%)
    pallas_call x1, Pallas kernels, per_device(): pl.pallas_call(reduce_kernel, out_shape=shape((W_DEV, 2 * KVC), F32), in_...  80 us
    pallas_call x1, Pallas kernels, per_device(): pl.pallas_call(gather_kernel, out_shape=[shape((N_CTX, REACH, PIECE, HD),...  42.1 us
    pallas_call x1, Pallas kernels, per_device(): pl.pallas_call(attend_kernel, grid=(KVH,), out_shape=[shape((ROWS, KVH *...  9.25 us
    unnamed x19, local copies, waits for them, and re-layouts  6.76 us

profile of v1, /device:TPU:1, one launch (start us, length us, event | category | flops | bytes accessed | tf_op | source)
XLA Modules:
  0.0 140.3 jit_solution(9150399093509106148)
XLA Ops:
  0.6 0.0 copy-start.8
  0.6 0.6 copy-done.8
  1.3 0.0 copy-start.4
  1.3 0.9 copy-done.4
  2.2 0.0 copy-start.5
  2.2 0.9 copy-done.5
  3.1 0.0 copy-start.6
  3.1 0.7 copy-done.6
  3.8 0.0 copy-start.7
  3.8 0.7 copy-done.7
  4.4 0.0 copy-start
  4.4 1.5 %prep.1 = (bf16[32,2,16,128]{3,2,1,0:T(8,128)(2,1)S(1)}, f32[128,128]{1,0:T(8,128)S(1)}, f32[128,128]{1,0:T(8,128)S(1)}, s32[1,64]{1,0:T(1,128)S(1)}) custom-call(s32[1,64]{1,0:T(1,128)S(1)} %copy-done.6, s32[1,32]{1,0:T(1,128)S(1)} %copy-done.7, f32[1,128]{1,0:T(1,128)S(1)} %copy-done.8, bf16[128,512]{1,0:T(8,128)(2,1)S(1)} %copy-done.4, ...), custom_call_target="tpu_custom_call" | custom-call | tf_op jit(solution)/shard_map/prep/pallas_call | solution.py:374
  5.9 0.0 copy-start.2
  5.9 1.1 copy-done.2
  7.0 42.1 %gather.1 = (bf16[32,8,16,128]{3,2,1,0:T(8,128)(2,1)S(1)}, bf16[8,128,384]{2,1,0:T(8,128)(2,1)S(1)}) custom-call(s32[1,64]{1,0:T(1,128)S(1)} %copy-done.6, s32[1,64]{1,0:T(1,128)S(1)} %get-tuple-element.11.slot_ref, bf16[32,2,16,128]{3,2,1,0:T(8,128)(2,1)S(1)} %get-tuple-element.12.pack_ref, bf16[128,3072]{1,0:T(8,128)(2,1)S(1)} %copy-done.2), custom_call_target="tpu_custom_call" | custom-call | tf_op jit(solution)/shard_map/gather/pallas_call | solution.py:388
  49.1 0.0 copy-done
  49.1 0.0 copy-start.1
  49.1 1.2 copy-done.1
  50.3 0.0 copy-start.3
  50.3 9.2 %attend.1 = (bf16[128,4096]{1,0:T(8,128)(2,1)}, bf16[2,4,4,8,16,128]{5,4,3,2,1,0:T(8,128)(2,1)S(1)}, f32[2,128,512]{2,1,0:T(8,128)S(1)}) custom-call(s32[1,64]{1,0:T(1,128)S(1)} %copy-done.6, s32[1,32]{1,0:T(1,128)S(1)} %copy-done.7, bf16[128,4096]{1,0:T(8,128)(2,1)S(1)} %copy-done, bf16[128,4096]{1,0:T(8,128)(2,1)S(1)} %copy-done.1, ...), custom_call_target="tpu_custom_call" | custom-call | tf_op jit(solution)/shard_map/attend/pallas_call | solution.py:411
  59.6 0.0 copy-done.3
  59.6 80.0 %reduce.1 = f32[12,1024]{1,0:T(8,128)S(1)} custom-call(s32[1,64]{1,0:T(1,128)S(1)} %copy-done.6, s32[1,64]{1,0:T(1,128)S(1)} %get-tuple-element.11.slot_ref, bf16[32,8,16,128]{3,2,1,0:T(8,128)(2,1)S(1)} %bitcast.3, f32[2,128,512]{2,1,0:T(8,128)S(1)} %get-tuple-element.18.own_ref, f32[128,128]{1,0:T(8,128)S(1)} %get-tuple-element.14.cos_ref, ...), custom_call_target="tpu_custom_call" | custom-call | tf_op jit(solution)/shard_map/reduce/pallas_call | solution.py:442
  139.6 0.6 copy.12
Async XLA Ops:
  0.6 0.7 copy-start.8
  1.3 0.9 copy-start.4
  2.2 0.9 copy-start.5
  3.1 0.7 copy-start.6
  3.8 0.7 copy-start.7
  4.4 44.7 %copy-start = (bf16[128,4096]{1,0:T(8,128)(2,1)S(1)}, bf16[128,4096]{1,0:T(8,128)(2,1)}, u32[]{:S(2)}) copy-start(bf16[128,4096]{1,0:T(8,128)(2,1)} %q_ref.1) | copy-start | bytes 3145732
  5.9 1.1 copy-start.2
  49.1 1.2 copy-start.1
  50.3 9.3 %copy-start.3 = (bf16[384,384]{1,0:T(8,128)(2,1)S(1)}, bf16[384,384]{1,0:T(8,128)(2,1)}, u32[]{:S(2)}) copy-start(bf16[384,384]{1,0:T(8,128)(2,1)} %constant.5.clone.perm_ref) | copy-start | bytes 884740

commit v2 on v0

v2 whole, which is shorter than its diff:
```python
import functools

import jax
import jax.numpy as jnp
import numpy as np
from jax import lax
from jax.experimental import pallas as pl
from jax.experimental.pallas import tpu as pltpu
from jax.sharding import PartitionSpec as P

MESH = pl.DeviceIdType.MESH
BF16 = jnp.bfloat16
F32 = jnp.float32
I32 = jnp.int32

KVH = 4
G = 8
HD = 128
ROT = 64
ROPE_BASE = 10000000.0
SPAN = 64
BACK = 4
ROWS = 2 * SPAN
KEYS = (BACK + 1) * SPAN
N_CTX = 32
N_DP = 8
N_X = 4
N_Z = 8
SLOTS = 2 * N_CTX
NDOC = 32
KVC = KVH * HD
PIECE = 16
N_ROW = SPAN // PIECE
N_PIECE = N_ROW * KVH
REACH = 2 * BACK
DW = 3072
W_DP = DW // N_DP
W_DEV = W_DP // N_CTX
W_X = W_DP // N_X
CHUNKS = 4
W_COL = 2 * KVC // CHUNKS
MASKED = -1e30
SCALE = HD**-0.5
VMEM_LIMIT = 60 * 1024 * 1024

NT = (((1,), (1,)), ((), ()))
TN = (((0,), (0,)), ((), ()))


def rope_lanes():
    half = ROT // 2
    freq = ROPE_BASE ** (-(np.arange(half, dtype=np.float64) * 2.0 / ROT))
    row = np.zeros((1, HD), np.float32)
    row[0, :half] = freq
    row[0, half:ROT] = freq
    return row


def feature_order():
    order = np.arange(W_DP).reshape(N_Z, N_X, W_DEV).transpose(1, 0, 2).reshape(-1)
    return np.eye(W_DP, dtype=np.float32)[order]


def swap_halves(x):
    lane = lax.broadcasted_iota(I32, x.shape, 1)
    return jnp.where(lane < ROT // 2, pltpu.roll(x, HD - ROT // 2, 1), pltpu.roll(x, ROT // 2, 1))


def begin_of(pos, len_ref):
    def step(d, carry):
        start, begin = carry
        return start + len_ref[0, d], jnp.where(pos >= start, start, begin)

    _, begin = lax.fori_loop(0, NDOC, step, (jnp.int32(0), jnp.zeros_like(pos)), unroll=True)
    return begin


def loop(first, last, body):
    def step(k, carry):
        body(k)
        return carry

    lax.fori_loop(first, last, step, 0)


def remote(src, dst, send, recv, device):
    return pltpu.make_async_remote_copy(
        src_ref=src, dst_ref=dst, send_sem=send, recv_sem=recv, device_id=device, device_id_type=MESH
    )


def lanes(at, size):
    return pl.ds(pl.multiple_of(at, HD), size)


def kernel(
    span_h, len_h, freq_h, perm_h, q_h, k_h, v_h, do_h, in_h, dq_h, out_ref,
    span, lens, slot_of, take, give,
    slot_v, freq, perm, q, keys, vals, do, cos, sin, bias, qrot, dq,
    pack, held, chosen, win, part, own, landed, total, back, x_in, xt,
    grads, wsend, xland, zsend, zland,
    local, send1, recv1, send2, recv2, send3, recv3, send4, recv4, send5, recv5,
    send6, recv6, send7, recv7, send8, recv8, send9, recv9,
):
    dp, me = lax.axis_index("dp"), lax.axis_index("ctx")
    z, x = me // N_X, lax.rem(me, N_X)
    sib = dp + 1 - 2 * lax.rem(dp, 2)
    ctx_peer = lambda k: lax.rem(me + k, N_CTX)
    dp_peer = lambda k: lax.rem(dp + k, N_DP)
    y_peer = lambda k: lax.rem(dp + 2 * k, N_DP)
    sib_peer = lambda k: lax.rem(sib + 2 * k, N_DP)
    x_peer = lambda k: lax.rem(x + k, N_X)
    z_peer = lambda k: lax.rem(z + k, N_Z)
    piece_here = lax.rem(z, N_ROW) * KVH + x

    def near(k):
        dz, dx = k // N_X, lax.rem(k, N_X)
        two = jnp.where(lax.rem(dx, 2) == 0, 2, N_Z - 2)
        return jnp.where(dz == 2, two, jnp.where(dz == 3, N_Z - 1, dz)), dx

    def reader(k):
        dz, dx = near(k)
        return lax.rem(z + dz, N_Z) * N_X + lax.rem(x + dx, N_X)

    def holder(k):
        dz, dx = near(k)
        return lax.rem(z + N_Z - dz, N_Z) * N_X + lax.rem(x + N_X - dx, N_X)

    def piece_of(device):
        return lax.rem(device, N_PIECE)

    own_cols = lanes(dp * W_DP, W_DP)
    fetches = [
        pltpu.make_async_copy(src, dst, local.at[n])
        for n, (src, dst) in enumerate([
            (span_h, span), (len_h, lens), (freq_h, freq), (k_h, keys), (v_h, vals),
            (q_h, q), (do_h, do), (perm_h, perm), (in_h.at[:, own_cols], x_in.at[dp]),
        ])
    ]
    for copy in fetches:
        copy.start()
    barrier = pltpu.get_barrier_semaphore()

    def greet(device):
        pl.semaphore_signal(barrier, inc=1, device_id=device, device_id_type=MESH)

    loop(1, N_CTX, lambda k: greet((dp, ctx_peer(k))))
    loop(1, N_DP, lambda k: greet((dp_peer(k), me)))

    for copy in fetches[:5]:
        copy.wait()
    lane_row = lax.broadcasted_iota(I32, (1, HD), 1)
    slots = jnp.zeros((1, HD), I32)
    for n in range(SLOTS):
        slots = jnp.where(lane_row == span[0, n], n, slots)
    slot_v[...] = slots
    slot_copy = pltpu.make_async_copy(slot_v, slot_of, local.at[9])
    slot_copy.start()
    row = lax.broadcasted_iota(I32, (ROWS, HD), 0)
    lane = lax.broadcasted_iota(I32, (ROWS, HD), 1)
    mine = (span[0, 2 * me], span[0, 2 * me + 1])
    pos = jnp.where(row >= SPAN, mine[1] * SPAN + row - SPAN, mine[0] * SPAN + row)
    rel = (pos - begin_of(pos, lens)).astype(F32)
    angle = rel * freq[...]
    sine = jnp.sin(angle)
    cos[...] = jnp.where(lane < ROT, jnp.cos(angle), 1.0)
    sin[...] = jnp.where(lane < ROT // 2, -sine, jnp.where(lane < ROT, sine, 0.0))
    for j in range(KVH):
        k = keys[:, j * HD : (j + 1) * HD].astype(F32)
        k = (k * cos[...] + swap_halves(k) * sin[...]).astype(BF16)
        v = vals[:, j * HD : (j + 1) * HD]
        for s in range(2):
            for r in range(N_ROW):
                at = s * SPAN + r * PIECE
                pack[r * KVH + j, s, 0] = k[at : at + PIECE]
                pack[r * KVH + j, s, 1] = v[at : at + PIECE]
    slot_copy.wait()
    pl.semaphore_wait(barrier, N_CTX - 1 + N_DP - 1)

    def copy1(src, owner, peer):
        return remote(
            pack.at[piece_of(src)], held.at[pl.ds(2 * owner, 2)], send1.at[src], recv1.at[owner], (dp, peer)
        )

    def copy5(src, owner, peer):
        cols = lanes(src * W_DP, W_DP)
        return remote(in_h.at[:, cols], x_in.at[owner], send5.at[src], recv5.at[owner], (peer, me))

    loop(1, N_CTX, lambda k: copy1(ctx_peer(k), me, ctx_peer(k)).start())
    loop(1, N_DP, lambda k: copy5(dp_peer(k), dp, dp_peer(k)).start())
    held[pl.ds(2 * me, 2)] = pack[piece_here]

    def fill(slot):
        at = span[0, slot]
        for w in range(BACK):
            take[slot * BACK + w] = slot_of[0, jnp.maximum(at - BACK + w, 0)]
            later = at + 1 + w
            source = slot_of[0, jnp.minimum(later, SLOTS - 1)] * BACK + (BACK - 1 - w)
            give[slot * BACK + w] = jnp.where(later < SLOTS, source, N_CTX * REACH)

    loop(0, SLOTS, fill)
    for s in range(2):
        lane8 = lax.broadcasted_iota(I32, (8, HD), 1)
        qpos = mine[s] * SPAN + jnp.where(lane8 >= SPAN, lane8 - SPAN, lane8)
        qbegin = begin_of(qpos, lens)
        n = lax.broadcasted_iota(I32, (KEYS, HD), 0)
        r, w, t = n >> 6, (n >> 4) & 3, n & 15
        earlier = (mine[s] - BACK + w) * SPAN + r * PIECE + t
        kpos = jnp.where(n < BACK * SPAN, earlier, mine[s] * SPAN + (n - BACK * SPAN))
        allowed = (kpos <= qpos[0:1]) & (kpos >= qbegin[0:1])
        bias[s] = jnp.where(allowed, 0.0, MASKED)
    fetches[5].wait()

    def rotate(h):
        v = q[:, lanes(h * HD, HD)].astype(F32)
        qrot[:, lanes(h * HD, HD)] = (v * cos[...] + swap_halves(v) * sin[...]).astype(BF16)

    loop(0, KVH * G, rotate)
    empty = jnp.zeros((REACH, 2, PIECE, HD), BF16)

    def clear(dz, dx):
        device = lax.rem(z + dz, N_Z) * N_X + lax.rem(x + dx, N_X)
        landed[pl.ds(REACH * device, REACH)] = empty

    loop(0, 12, lambda k: clear(3 + k // N_X, lax.rem(k, N_X)))
    loop(0, 2, lambda k: clear(2, 2 * k + 1))
    loop(0, 2, lambda k: clear(6, 2 * k))
    landed[N_CTX * REACH] = jnp.zeros((2, PIECE, HD), BF16)
    loop(1, N_CTX, lambda k: copy1(me, ctx_peer(k), ctx_peer(k)).wait_recv())

    def choose(s, k):
        device = reader(k)
        for w in range(BACK):
            chosen[s, k, w] = held[take[device * REACH + s * BACK + w]]

    def copy2(s, k, peer, piece):
        return remote(chosen.at[s, k], win.at[s, piece], send2.at[s, k], recv2.at[s, k], (dp, peer))

    for s in range(2):

        def serve(k, s=s):
            choose(s, k)
            copy2(s, k, reader(k), piece_here).start()

        loop(1, N_PIECE, serve)
        choose(s, 0)
        win[s, piece_here] = chosen[s, 0]
    fetches[6].wait()
    fetches[7].wait()
    fetches[8].wait()
    loop(1, N_DP, lambda k: copy5(dp, dp_peer(k), dp_peer(k)).wait_recv())
    for d in range(N_DP):
        turned = lax.dot_general(perm[...], x_in[d], NT, preferred_element_type=F32)
        xt[:, d * ROWS : (d + 1) * ROWS] = turned.astype(BF16)

    def copy3(s, k, src, owner, peer):
        return remote(
            part.at[s, src],
            landed.at[pl.ds(REACH * owner + BACK * s, BACK)],
            send3.at[s, k],
            recv3.at[s, k],
            (dp, peer),
        )

    for s in range(2):
        loop(1, N_PIECE, lambda k, s=s: copy2(s, k, holder(k), piece_of(holder(k))).wait_recv())
        rows = slice(s * SPAN, (s + 1) * SPAN)

        def attend(n, s=s, rows=rows):
            j = lax.rem(x + n, KVH)

            def window(kind):
                parts = [win[s, r * KVH + j, :, kind].reshape(BACK * PIECE, HD) for r in range(N_ROW)]
                parts += [pack[r * KVH + j, s, kind] for r in range(N_ROW)]
                return jnp.concatenate(parts, axis=0)

            def stacked(ref):
                parts = [ref[rows, lanes((j * G + g) * HD, HD)] for g in range(G)]
                return jnp.concatenate(parts, axis=0)

            k, v = window(0), window(1)
            qs, dos = stacked(qrot), stacked(do)
            mask = jnp.concatenate([bias[s]] * (G * SPAN // HD), axis=1)
            scores = lax.dot_general(k, qs, NT, preferred_element_type=F32)
            scores = scores * (SCALE * float(np.log2(np.e))) + mask
            weight = jnp.exp2(scores - jnp.max(scores, axis=0, keepdims=True))
            probs = weight * (1.0 / jnp.sum(weight, axis=0, keepdims=True))
            dprobs = lax.dot_general(v, dos, NT, preferred_element_type=F32)
            delta = jnp.sum(probs * dprobs, axis=0, keepdims=True)
            dscores = (probs * (dprobs - delta)).astype(BF16)
            low = probs.astype(BF16)
            dk = jnp.dot(dscores, qs, preferred_element_type=F32) * SCALE
            dv = jnp.dot(low, dos, preferred_element_type=F32)
            for kind, grad in ((0, dk), (1, dv)):
                earlier = grad[: BACK * SPAN].astype(BF16).reshape(N_ROW, BACK, PIECE, HD)
                for r in range(N_ROW):
                    part[s, r * KVH + j, :, kind] = earlier[r]
                own[kind, rows, lanes(j * HD, HD)] = grad[BACK * SPAN :]
            dx = lax.rem(N_X - n, N_X)

            def hand_over(dz):
                at = dz * N_X + dx

                @pl.when(at > 0)
                def _():
                    copy3(s, at, piece_of(holder(at)), me, holder(at)).start()

            loop(0, N_ROW, hand_over)
            dqt = lax.dot_general(k, dscores, TN, preferred_element_type=F32)
            turned = dqt.T * SCALE
            for g in range(G):
                u = turned[g * SPAN : (g + 1) * SPAN]
                u = u * cos[rows] - swap_halves(u) * sin[rows]
                dq[rows, lanes((j * G + g) * HD, HD)] = u.astype(BF16)

        loop(0, KVH, attend)
        landed[pl.ds(REACH * me + BACK * s, BACK)] = part[s, piece_here]
    dq_copy = pltpu.make_async_copy(dq, dq_h, local.at[10])
    dq_copy.start()
    for s in range(2):
        loop(1, N_PIECE, lambda k, s=s: copy3(s, k, piece_here, reader(k), reader(k)).wait_recv())

    def copy4(kind, src, owner, peer):
        return remote(
            total.at[kind, src], back.at[kind, owner], send4.at[kind, src], recv4.at[kind, owner], (dp, peer)
        )

    def sum_up(kind, device):
        for s in range(2):
            at = (2 * device + s) * BACK
            acc = landed[give[at], kind].astype(F32)
            for w in range(1, BACK):
                acc += landed[give[at + w], kind].astype(F32)
            total[kind, device, s] = acc.astype(BF16)

    for kind in range(2):

        def give_back(k, kind=kind):
            sum_up(kind, ctx_peer(k))
            copy4(kind, ctx_peer(k), me, ctx_peer(k)).start()

        loop(1, N_CTX, give_back)
        sum_up(kind, me)
        back[kind, me] = total[kind, me]

    def copy6(c, owner, peer):
        return remote(grads.at[owner, c], grads.at[owner, c], send6.at[c, peer], recv6.at[c, owner], (peer, me))

    def copy7(c, owner):
        return remote(grads.at[owner, c], grads.at[owner, c], send7.at[c, owner], recv7.at[c, owner], (sib, me))

    for kind in range(2):
        loop(1, N_CTX, lambda k, kind=kind: copy4(kind, me, ctx_peer(k), ctx_peer(k)).wait_recv())
        for half in range(2):
            c = 2 * kind + half
            for j in (2 * half, 2 * half + 1):
                for r in range(N_ROW):
                    for s in range(2):
                        rows = slice(s * SPAN + r * PIECE, s * SPAN + (r + 1) * PIECE)
                        piece = r * KVH + j
                        g = back[kind, piece, s].astype(F32) + back[kind, N_PIECE + piece, s].astype(F32)
                        g += own[kind, rows, j * HD : (j + 1) * HD]
                        if kind == 0:
                            g = g * cos[rows] - swap_halves(g) * sin[rows]
                        cols = slice((j - 2 * half) * HD, (j - 2 * half + 1) * HD)
                        grads[dp, c, rows, cols] = g.astype(BF16)
            loop(1, 4, lambda k, c=c: copy6(c, dp, y_peer(k)).start())
            copy7(c, dp).start()

    def copy8(c, src, owner, peer):
        return remote(wsend.at[c, src], xland.at[c, owner], send8.at[c, src], recv8.at[c, owner], (dp, z * N_X + peer))

    def copy9(c, src, owner, peer):
        return remote(zsend.at[c, src], zland.at[c, owner], send9.at[c, src], recv9.at[c, owner], (dp, peer * N_X + x))

    def forward(c):
        for k in range(1, 4):
            copy6(c, y_peer(k), y_peer(k)).wait_recv()
            copy7(c, y_peer(k)).start()

    def multiply(c):
        loop(0, 4, lambda k: copy7(c, sib_peer(k)).wait_recv())
        w = jnp.dot(xt[...], grads[:, c].reshape(N_DP * ROWS, W_COL), preferred_element_type=F32)
        wsend[c] = w.astype(BF16).reshape(N_X, W_X, W_COL)
        loop(1, N_X, lambda k: copy8(c, x_peer(k), x, x_peer(k)).start())
        xland[c, x] = wsend[c, x]

    def sum_x(c):
        loop(1, N_X, lambda k: copy8(c, x, x_peer(k), x_peer(k)).wait_recv())
        acc = xland[c, 0].astype(F32)
        for n in range(1, N_X):
            acc += xland[c, n].astype(F32)
        pad = jnp.zeros((PIECE - W_DEV, W_COL), F32)
        for n in range(N_Z):
            block = jnp.concatenate([acc[n * W_DEV : (n + 1) * W_DEV], pad], axis=0)
            zsend[c, n] = block.astype(BF16)
        loop(1, N_Z, lambda k: copy9(c, z_peer(k), z, z_peer(k)).start())
        zland[c, z] = zsend[c, z]

    def sum_z(c):
        loop(1, N_Z, lambda k: copy9(c, z, z_peer(k), z_peer(k)).wait_recv())
        acc = zland[c, 0].astype(F32)
        for n in range(1, N_Z):
            acc += zland[c, n].astype(F32)
        out_ref[:, c * W_COL : (c + 1) * W_COL] = acc[:W_DEV]

    forward(0)
    for c in range(CHUNKS):
        if c + 1 < CHUNKS:
            forward(c + 1)
        multiply(c)
    for c in range(CHUNKS):
        sum_x(c)
    for c in range(CHUNKS):
        sum_z(c)

    loop(1, N_CTX, lambda k: copy1(ctx_peer(k), me, ctx_peer(k)).wait_send())
    loop(1, N_DP, lambda k: copy5(dp_peer(k), dp, dp_peer(k)).wait_send())
    for s in range(2):
        loop(1, N_PIECE, lambda k, s=s: copy2(s, k, reader(k), piece_here).wait_send())
        loop(1, N_PIECE, lambda k, s=s: copy3(s, k, piece_of(holder(k)), me, holder(k)).wait_send())
    for kind in range(2):
        loop(1, N_CTX, lambda k, kind=kind: copy4(kind, ctx_peer(k), me, ctx_peer(k)).wait_send())
    for c in range(CHUNKS):
        loop(1, 4, lambda k, c=c: copy6(c, dp, y_peer(k)).wait_send())
        loop(0, 4, lambda k, c=c: copy7(c, y_peer(k)).wait_send())
        loop(1, N_X, lambda k, c=c: copy8(c, x_peer(k), x, x_peer(k)).wait_send())
        loop(1, N_Z, lambda k, c=c: copy9(c, z_peer(k), z, z_peer(k)).wait_send())
    dq_copy.wait()


def per_device(queries, keys, values, grad_out, inputs, span_map, doc_lengths):
    vmem, smem, dma = pltpu.VMEM, pltpu.SMEM, pltpu.SemaphoreType.DMA
    hbm = pl.BlockSpec(memory_space=pl.ANY)
    wide = KVH * G * HD
    tile = (PIECE, HD)
    return pl.pallas_call(
        kernel,
        out_shape=[
            jax.ShapeDtypeStruct((ROWS, wide), BF16),
            jax.ShapeDtypeStruct((W_DEV, 2 * KVC), F32),
        ],
        in_specs=[hbm] * 9,
        out_specs=[hbm, pl.BlockSpec(memory_space=pltpu.VMEM)],
        scratch_shapes=[
            smem((1, SLOTS), I32),
            smem((1, NDOC), I32),
            smem((1, HD), I32),
            smem((SLOTS * BACK,), I32),
            smem((SLOTS * BACK,), I32),
            vmem((1, HD), I32),
            vmem((1, HD), F32),
            vmem((W_DP, W_DP), BF16),
            vmem((ROWS, wide), BF16),
            vmem((ROWS, KVC), BF16),
            vmem((ROWS, KVC), BF16),
            vmem((ROWS, wide), BF16),
            vmem((ROWS, HD), F32),
            vmem((ROWS, HD), F32),
            vmem((2, KEYS, HD), F32),
            vmem((ROWS, wide), BF16),
            vmem((ROWS, wide), BF16),
            vmem((N_PIECE, 2, 2) + tile, BF16),
            vmem((SLOTS, 2) + tile, BF16),
            vmem((2, N_PIECE, BACK, 2) + tile, BF16),
            vmem((2, N_PIECE, BACK, 2) + tile, BF16),
            vmem((2, N_PIECE, BACK, 2) + tile, BF16),
            vmem((2, ROWS, KVC), F32),
            vmem((N_CTX * REACH + 1, 2) + tile, BF16),
            vmem((2, N_CTX, 2) + tile, BF16),
            vmem((2, N_CTX, 2) + tile, BF16),
            vmem((N_DP, ROWS, W_DP), BF16),
            vmem((W_DP, N_DP * ROWS), BF16),
            vmem((N_DP, CHUNKS, ROWS, W_COL), BF16),
            vmem((CHUNKS, N_X, W_X, W_COL), BF16),
            vmem((CHUNKS, N_X, W_X, W_COL), BF16),
            vmem((CHUNKS, N_Z, PIECE, W_COL), BF16),
            vmem((CHUNKS, N_Z, PIECE, W_COL), BF16),
            dma((11,)),
            dma((N_CTX,)), dma((N_CTX,)),
            dma((2, N_PIECE)), dma((2, N_PIECE)),
            dma((2, N_PIECE)), dma((2, N_PIECE)),
            dma((2, N_CTX)), dma((2, N_CTX)),
            dma((N_DP,)), dma((N_DP,)),
            dma((CHUNKS, N_DP)), dma((CHUNKS, N_DP)),
            dma((CHUNKS, N_DP)), dma((CHUNKS, N_DP)),
            dma((CHUNKS, N_X)), dma((CHUNKS, N_X)),
            dma((CHUNKS, N_Z)), dma((CHUNKS, N_Z)),
        ],
        compiler_params=pltpu.CompilerParams(
            collective_id=0, has_side_effects=True, vmem_limit_bytes=VMEM_LIMIT
        ),
        name="packed_backward",
    )(
        span_map, doc_lengths, jnp.asarray(rope_lanes()), jnp.asarray(feature_order(), BF16),
        queries, keys, values, grad_out, inputs,
    )


def solution(mesh):
    rows = P(("dp", "ctx"), None)
    return jax.shard_map(
        per_device,
        mesh=mesh,
        in_specs=(rows, rows, rows, rows, rows, P("dp", None), P("dp", None)),
        out_specs=(rows, rows),
        check_vma=False,
    )
```

time: 818 us -> 100 us (0.12)
  waiting for transfers between devices: 647 us -> 0 us
  local copies, waits for them, and re-layouts: 110 us -> 2.95 us
  Pallas kernels: 0 us -> 96.7 us
  other arithmetic: 20.5 us -> 0 us
  matrix products: 17.7 us -> 0 us
  between operations: 14.3 us -> 0.65 us
    unnamed x5 -> x0, waiting for transfers between devices: 284 us -> none
    reduce_scatter x1 -> x0, waiting for transfers between devices: 225 us -> none  [per_device(): lax.psum_scatter(partial_value, 'ctx', scatter_dimension=0, tiled=True)]
    all_gather x2 -> x0, waiting for transfers between devices: 139 us -> none  [the longest x1 76.5 us: per_device(): lax.all_gather(values, 'ctx', axis=0, tiled=True)]
    pallas_call x0 -> x1, Pallas kernels: none -> 96.7 us  [per_device(): pl.pallas_call(kernel, out_shape=[jax.ShapeDtypeStruct((ROWS, wide), BF16...]
    scatter x1 -> x0, local copies, waits for them, and re-layouts: 43.4 us -> none  [per_device(): partial_value = jnp.zeros((slot_count, half_rows * 2 * kv_cols), jnp.bflo...]
    reshape x7 -> x0, local copies, waits for them, and re-layouts: 18.8 us -> none  [the longest x1 10.6 us: per_device(): partial_value = partial_value.reshape(seq_rows, 2 * kv_cols)]
    dot_general x12 -> x0, matrix products: 17.7 us -> none  [the longest x1 6.3 us: per_device(): lax.dot_general(inputs, grads_low, (((0,), (0,)), ((), ())), preferred_el...]
    while x29 -> x0, local copies, waits for them, and re-layouts: 11.8 us -> none
  transfers between devices with their start and end apart: 4 -> 0, of which waited for: 4 -> 0; matrix products, arithmetic and copies ran while one was open for 4% -> 0% of each run, Pallas kernels for 0% -> 0%
where the time goes in v2:
time: 100 us
  Pallas kernels  96.7 us (97%)
  local copies, waits for them, and re-layouts  2.95 us (3%)
    pallas_call x1, Pallas kernels, per_device(): pl.pallas_call(kernel, out_shape=[jax.ShapeDtypeStruct((ROWS, wide), BF16...  96.7 us
    unnamed x4, local copies, waits for them, and re-layouts  2.95 us

profile of v2, /device:TPU:1, one launch (start us, length us, event | category | flops | bytes accessed | tf_op | source)
XLA Modules:
  0.0 100.3 jit_solution(11320858345037388343)
XLA Ops:
  0.6 96.7 %packed_backward.1 = (bf16[128,4096]{1,0:T(8,128)(2,1)}, f32[12,1024]{1,0:T(8,128)}) custom-call(s32[1,64]{1,0:T(1,128)} %span_h.1, s32[1,32]{1,0:T(1,128)} %len_h.1, f32[1,128]{1,0:T(1,128)} %constant.4.clone.freq_h, bf16[384,384]{1,0:T(8,128)(2,1)} %constant.5.clone.perm_h, bf16[128,4096]{1,0:T(8,128)(2,1)} %q_h.1, bf16[128,512]{1,0:T(8,128)(2,1)} %k_h.1, ...), custom_call_target="tpu_custom_call" | custom-call | tf_op jit(solution)/shard_map/packed_backward/pallas_call | solution.py:437
  97.3 0.0 copy-start
  97.4 2.3 %copy.13 = bf16[128,4096]{1,0:T(8,128)(2,1)} copy(bf16[128,4096]{1,0:T(8,128)(2,1)} %get-tuple-element.4) | data formatting | bytes 2097152
  99.7 0.0 copy-done
  99.7 0.6 copy.14
Async XLA Ops:
  97.3 2.3 %copy-start = (f32[12,1024]{1,0:T(8,128)S(1)}, f32[12,1024]{1,0:T(8,128)}, u32[]{:S(2)}) copy-start(f32[12,1024]{1,0:T(8,128)} %get-tuple-element.5) | copy-start | bytes 147460

commit v3 on v2

--- a/solution.py
+++ b/solution.py
@@ -39,6 +39,8 @@
 W_X = W_DP // N_X
 CHUNKS = 4
 W_COL = 2 * KVC // CHUNKS
+N_Y = N_DP // 2
+LINE = 4
 MASKED = -1e30
 SCALE = HD**-0.5
 VMEM_LIMIT = 60 * 1024 * 1024
@@ -50,10 +52,7 @@
 def rope_lanes():
     half = ROT // 2
     freq = ROPE_BASE ** (-(np.arange(half, dtype=np.float64) * 2.0 / ROT))
-    row = np.zeros((1, HD), np.float32)
-    row[0, :half] = freq
-    row[0, half:ROT] = freq
-    return row
+    return np.tile(freq.astype(np.float32), HD // half)[None]
 
 
 def feature_order():
@@ -89,6 +88,24 @@
     )
 
 
+def rope_tables(pos, lens, freq, cos, sin):
+    rel = (pos - begin_of(pos, lens)).astype(F32)
+    angle = rel * freq[...]
+    packed_cos, packed_sin = jnp.cos(angle), jnp.sin(angle)
+    lane = lax.broadcasted_iota(I32, pos.shape, 1)
+    half, rows = ROT // 2, pos.shape[0]
+
+    def turn(v, shift):
+        shift = shift % HD
+        return pltpu.roll(v, shift, 1) if shift else v
+
+    for n in range(HD // half):
+        pair = lambda v: (turn(v, -half * n), turn(v, half - half * n))
+        (c0, c1), (s0, s1) = pair(packed_cos), pair(packed_sin)
+        cos[n * rows : (n + 1) * rows] = jnp.where(lane < half, c0, jnp.where(lane < ROT, c1, 1.0))
+        sin[n * rows : (n + 1) * rows] = jnp.where(lane < half, -s0, jnp.where(lane < ROT, s1, 0.0))
+
+
 def lanes(at, size):
     return pl.ds(pl.multiple_of(at, HD), size)
 
@@ -96,20 +113,23 @@
 def kernel(
     span_h, len_h, freq_h, perm_h, q_h, k_h, v_h, do_h, in_h, dq_h, out_ref,
     span, lens, slot_of, take, give,
-    slot_v, freq, perm, q, keys, vals, do, cos, sin, bias, qrot, dq,
-    pack, held, chosen, win, part, own, landed, total, back, x_in, xt,
-    grads, wsend, xland, zsend, zland,
-    local, send1, recv1, send2, recv2, send3, recv3, send4, recv4, send5, recv5,
+    slot_v, freq, perm, q, keys, vals, do, feats, cos, sin, bias, qrot, dq,
+    pack, held, chosen, win, part, own, landed, total, back, turned, xta, xtb,
+    grads, wsend, wland, zsend, zland,
+    local, send1, recv1, send2, recv2, send3, recv3, send4, recv4, send5, recv5, send0, recv0,
     send6, recv6, send7, recv7, send8, recv8, send9, recv9,
 ):
     dp, me = lax.axis_index("dp"), lax.axis_index("ctx")
     z, x = me // N_X, lax.rem(me, N_X)
-    sib = dp + 1 - 2 * lax.rem(dp, 2)
+    y, core = dp // 2, lax.rem(dp, 2)
+    sib = dp + 1 - 2 * core
+    team = 2 * x + core
     ctx_peer = lambda k: lax.rem(me + k, N_CTX)
     dp_peer = lambda k: lax.rem(dp + k, N_DP)
     y_peer = lambda k: lax.rem(dp + 2 * k, N_DP)
     sib_peer = lambda k: lax.rem(sib + 2 * k, N_DP)
     x_peer = lambda k: lax.rem(x + k, N_X)
+    team_peer = lambda k: lax.rem(team + k, 2 * N_X)
     z_peer = lambda k: lax.rem(z + k, N_Z)
     piece_here = lax.rem(z, N_ROW) * KVH + x
 
@@ -129,12 +149,11 @@
     def piece_of(device):
         return lax.rem(device, N_PIECE)
 
-    own_cols = lanes(dp * W_DP, W_DP)
     fetches = [
         pltpu.make_async_copy(src, dst, local.at[n])
         for n, (src, dst) in enumerate([
-            (span_h, span), (len_h, lens), (freq_h, freq), (k_h, keys), (v_h, vals),
-            (q_h, q), (do_h, do), (perm_h, perm), (in_h.at[:, own_cols], x_in.at[dp]),
+            (k_h, keys), (v_h, vals), (span_h, span), (len_h, lens), (freq_h, freq),
+            (perm_h, perm), (in_h, feats), (q_h, q), (do_h, do),
         ])
     ]
     for copy in fetches:
@@ -146,8 +165,56 @@
 
     loop(1, N_CTX, lambda k: greet((dp, ctx_peer(k))))
     loop(1, N_DP, lambda k: greet((dp_peer(k), me)))
-
-    for copy in fetches[:5]:
+    loop(1, N_X, lambda k: greet((sib, z * N_X + x_peer(k))))
+    for copy in fetches[:2]:
+        copy.wait()
+    for s in range(2):
+        for r in range(N_ROW):
+            rows = slice(s * SPAN + r * PIECE, s * SPAN + (r + 1) * PIECE)
+            for j in range(KVH):
+                cols = slice(j * HD, (j + 1) * HD)
+                pack[r * KVH + j, s, 0] = keys[rows, cols]
+                pack[r * KVH + j, s, 1] = vals[rows, cols]
+    pl.semaphore_wait(barrier, N_CTX - 1 + N_DP - 1 + N_X - 1)
+
+    def copy1(src, owner, peer):
+        return remote(
+            pack.at[piece_of(src)], held.at[pl.ds(2 * owner, 2)], send1.at[src], recv1.at[owner], (dp, peer)
+        )
+
+    loop(1, N_CTX, lambda k: copy1(ctx_peer(k), me, ctx_peer(k)).start())
+    held[pl.ds(2 * me, 2)] = pack[piece_here]
+
+    def copy5(src, owner, peer):
+        return remote(
+            turned.at[src // 2, lax.rem(src, 2)],
+            xta.at[:, :, lanes(owner * ROWS, ROWS)],
+            send5.at[src],
+            recv5.at[owner],
+            (peer, me),
+        )
+
+    def copy0(src, owner, peer):
+        device = (dp - core + lax.rem(peer, 2), z * N_X + peer // 2)
+        return remote(
+            turned.at[:, lax.rem(src, 2), src // 2],
+            xtb.at[:, :, lanes(owner * ROWS, ROWS)],
+            send0.at[src],
+            recv0.at[owner],
+            device,
+        )
+
+    fetches[5].wait()
+    fetches[6].wait()
+    for d in range(N_DP):
+        w = lax.dot_general(perm[...], feats[:, d * W_DP : (d + 1) * W_DP], NT, preferred_element_type=F32)
+        turned[d // 2, d % 2] = w.astype(BF16).reshape(N_X, W_X, ROWS)
+    loop(1, N_DP, lambda k: copy5(dp_peer(k), dp, dp_peer(k)).start())
+    loop(1, 2 * N_X, lambda k: copy0(team_peer(k), team, team_peer(k)).start())
+    xta[:, :, lanes(dp * ROWS, ROWS)] = turned[y, core]
+    xtb[:, :, lanes(team * ROWS, ROWS)] = turned[:, core, x]
+
+    for copy in fetches[2:5]:
         copy.wait()
     lane_row = lax.broadcasted_iota(I32, (1, HD), 1)
     slots = jnp.zeros((1, HD), I32)
@@ -156,39 +223,19 @@
     slot_v[...] = slots
     slot_copy = pltpu.make_async_copy(slot_v, slot_of, local.at[9])
     slot_copy.start()
-    row = lax.broadcasted_iota(I32, (ROWS, HD), 0)
-    lane = lax.broadcasted_iota(I32, (ROWS, HD), 1)
     mine = (span[0, 2 * me], span[0, 2 * me + 1])
-    pos = jnp.where(row >= SPAN, mine[1] * SPAN + row - SPAN, mine[0] * SPAN + row)
-    rel = (pos - begin_of(pos, lens)).astype(F32)
-    angle = rel * freq[...]
-    sine = jnp.sin(angle)
-    cos[...] = jnp.where(lane < ROT, jnp.cos(angle), 1.0)
-    sin[...] = jnp.where(lane < ROT // 2, -sine, jnp.where(lane < ROT, sine, 0.0))
-    for j in range(KVH):
-        k = keys[:, j * HD : (j + 1) * HD].astype(F32)
-        k = (k * cos[...] + swap_halves(k) * sin[...]).astype(BF16)
-        v = vals[:, j * HD : (j + 1) * HD]
-        for s in range(2):
-            for r in range(N_ROW):
-                at = s * SPAN + r * PIECE
-                pack[r * KVH + j, s, 0] = k[at : at + PIECE]
-                pack[r * KVH + j, s, 1] = v[at : at + PIECE]
+    for s in range(2):
+        own_rows = SPAN // 4
+        row = lax.broadcasted_iota(I32, (own_rows, HD), 0)
+        group = lax.broadcasted_iota(I32, (own_rows, HD), 1) >> 5
+        at = pl.ds(BACK * SPAN, SPAN)
+        rope_tables(mine[s] * SPAN + group * own_rows + row, lens, freq, cos.at[s, at], sin.at[s, at])
+        row = lax.broadcasted_iota(I32, (SPAN, HD), 0)
+        group = lax.broadcasted_iota(I32, (SPAN, HD), 1) >> 5
+        pos = (mine[s] - BACK + (row >> 4)) * SPAN + group * PIECE + (row & 15)
+        at = pl.ds(0, BACK * SPAN)
+        rope_tables(pos, lens, freq, cos.at[s, at], sin.at[s, at])
     slot_copy.wait()
-    pl.semaphore_wait(barrier, N_CTX - 1 + N_DP - 1)
-
-    def copy1(src, owner, peer):
-        return remote(
-            pack.at[piece_of(src)], held.at[pl.ds(2 * owner, 2)], send1.at[src], recv1.at[owner], (dp, peer)
-        )
-
-    def copy5(src, owner, peer):
-        cols = lanes(src * W_DP, W_DP)
-        return remote(in_h.at[:, cols], x_in.at[owner], send5.at[src], recv5.at[owner], (peer, me))
-
-    loop(1, N_CTX, lambda k: copy1(ctx_peer(k), me, ctx_peer(k)).start())
-    loop(1, N_DP, lambda k: copy5(dp_peer(k), dp, dp_peer(k)).start())
-    held[pl.ds(2 * me, 2)] = pack[piece_here]
 
     def fill(slot):
         at = span[0, slot]
@@ -209,11 +256,14 @@
         kpos = jnp.where(n < BACK * SPAN, earlier, mine[s] * SPAN + (n - BACK * SPAN))
         allowed = (kpos <= qpos[0:1]) & (kpos >= qbegin[0:1])
         bias[s] = jnp.where(allowed, 0.0, MASKED)
-    fetches[5].wait()
+    fetches[7].wait()
 
     def rotate(h):
-        v = q[:, lanes(h * HD, HD)].astype(F32)
-        qrot[:, lanes(h * HD, HD)] = (v * cos[...] + swap_halves(v) * sin[...]).astype(BF16)
+        for s in range(2):
+            rows = slice(s * SPAN, (s + 1) * SPAN)
+            v = q[rows, lanes(h * HD, HD)].astype(F32)
+            v = v * cos[s, BACK * SPAN :] + swap_halves(v) * sin[s, BACK * SPAN :]
+            qrot[rows, lanes(h * HD, HD)] = v.astype(BF16)
 
     loop(0, KVH * G, rotate)
     empty = jnp.zeros((REACH, 2, PIECE, HD), BF16)
@@ -245,13 +295,7 @@
         loop(1, N_PIECE, serve)
         choose(s, 0)
         win[s, piece_here] = chosen[s, 0]
-    fetches[6].wait()
-    fetches[7].wait()
     fetches[8].wait()
-    loop(1, N_DP, lambda k: copy5(dp, dp_peer(k), dp_peer(k)).wait_recv())
-    for d in range(N_DP):
-        turned = lax.dot_general(perm[...], x_in[d], NT, preferred_element_type=F32)
-        xt[:, d * ROWS : (d + 1) * ROWS] = turned.astype(BF16)
 
     def copy3(s, k, src, owner, peer):
         return remote(
@@ -278,7 +322,8 @@
                 parts = [ref[rows, lanes((j * G + g) * HD, HD)] for g in range(G)]
                 return jnp.concatenate(parts, axis=0)
 
-            k, v = window(0), window(1)
+            k, v = window(0).astype(F32), window(1)
+            k = (k * cos[s] + swap_halves(k) * sin[s]).astype(BF16)
             qs, dos = stacked(qrot), stacked(do)
             mask = jnp.concatenate([bias[s]] * (G * SPAN // HD), axis=1)
             scores = lax.dot_general(k, qs, NT, preferred_element_type=F32)
@@ -307,10 +352,10 @@
 
             loop(0, N_ROW, hand_over)
             dqt = lax.dot_general(k, dscores, TN, preferred_element_type=F32)
-            turned = dqt.T * SCALE
+            upright = dqt.T * SCALE
             for g in range(G):
-                u = turned[g * SPAN : (g + 1) * SPAN]
-                u = u * cos[rows] - swap_halves(u) * sin[rows]
+                u = upright[g * SPAN : (g + 1) * SPAN]
+                u = u * cos[s, BACK * SPAN :] - swap_halves(u) * sin[s, BACK * SPAN :]
                 dq[rows, lanes((j * G + g) * HD, HD)] = u.astype(BF16)
 
         loop(0, KVH, attend)
@@ -343,53 +388,73 @@
         sum_up(kind, me)
         back[kind, me] = total[kind, me]
 
-    def copy6(c, owner, peer):
-        return remote(grads.at[owner, c], grads.at[owner, c], send6.at[c, peer], recv6.at[c, owner], (peer, me))
+    def line(half, k):
+        if half == 0:
+            return y_peer(k), (y_peer(k), me)
+        return 2 * x_peer(k) + core, (dp, z * N_X + x_peer(k))
+
+    def across(half, k):
+        return sib_peer(k) if half == 0 else 2 * x_peer(k) + 1 - core
+
+    def copy6(c, owner, k):
+        _, device = line(c % 2, k)
+        return remote(grads.at[c, owner], grads.at[c, owner], send6.at[c, k], recv6.at[c, owner], device)
 
     def copy7(c, owner):
-        return remote(grads.at[owner, c], grads.at[owner, c], send7.at[c, owner], recv7.at[c, owner], (sib, me))
-
-    for kind in range(2):
-        loop(1, N_CTX, lambda k, kind=kind: copy4(kind, me, ctx_peer(k), ctx_peer(k)).wait_recv())
-        for half in range(2):
-            c = 2 * kind + half
-            for j in (2 * half, 2 * half + 1):
-                for r in range(N_ROW):
-                    for s in range(2):
-                        rows = slice(s * SPAN + r * PIECE, s * SPAN + (r + 1) * PIECE)
-                        piece = r * KVH + j
-                        g = back[kind, piece, s].astype(F32) + back[kind, N_PIECE + piece, s].astype(F32)
-                        g += own[kind, rows, j * HD : (j + 1) * HD]
-                        if kind == 0:
-                            g = g * cos[rows] - swap_halves(g) * sin[rows]
-                        cols = slice((j - 2 * half) * HD, (j - 2 * half + 1) * HD)
-                        grads[dp, c, rows, cols] = g.astype(BF16)
-            loop(1, 4, lambda k, c=c: copy6(c, dp, y_peer(k)).start())
-            copy7(c, dp).start()
-
-    def copy8(c, src, owner, peer):
-        return remote(wsend.at[c, src], xland.at[c, owner], send8.at[c, src], recv8.at[c, owner], (dp, z * N_X + peer))
+        return remote(grads.at[c, owner], grads.at[c, owner], send7.at[c, owner], recv7.at[c, owner], (sib, me))
+
+    member = lambda c: (dp, team)[c % 2]
+
+    def assemble(c):
+        kind, half = c // 2, c % 2
+        for n in range(2):
+            j = 2 * half + n
+            for r in range(N_ROW):
+                for s in range(2):
+                    rows = slice(s * SPAN + r * PIECE, s * SPAN + (r + 1) * PIECE)
+                    piece = r * KVH + j
+                    g = back[kind, piece, s].astype(F32) + back[kind, N_PIECE + piece, s].astype(F32)
+                    g += own[kind, rows, j * HD : (j + 1) * HD]
+                    if kind == 0:
+                        at = slice(BACK * SPAN + r * PIECE, BACK * SPAN + (r + 1) * PIECE)
+                        g = g * cos[s, at] - swap_halves(g) * sin[s, at]
+                    grads[c, member(c), rows, n * HD : (n + 1) * HD] = g.astype(BF16)
+        loop(1, LINE, lambda k: copy6(c, member(c), k).start())
+        copy7(c, member(c)).start()
+
+    def forward(c):
+        for k in range(1, LINE):
+            owner, _ = line(c % 2, k)
+            copy6(c, owner, k).wait_recv()
+            copy7(c, owner).start()
+
+    def rest(half, k):
+        if half == 0:
+            return x_peer(k), (dp, z * N_X + x_peer(k))
+        return y_peer(k) // 2, (y_peer(k), me)
+
+    place = lambda c: (x, y)[c % 2]
+
+    def copy8(c, src, owner, k):
+        _, device = rest(c % 2, k)
+        return remote(wsend.at[c, src], wland.at[c, owner], send8.at[c, src], recv8.at[c, owner], device)
 
     def copy9(c, src, owner, peer):
         return remote(zsend.at[c, src], zland.at[c, owner], send9.at[c, src], recv9.at[c, owner], (dp, peer * N_X + x))
 
-    def forward(c):
-        for k in range(1, 4):
-            copy6(c, y_peer(k), y_peer(k)).wait_recv()
-            copy7(c, y_peer(k)).start()
-
     def multiply(c):
-        loop(0, 4, lambda k: copy7(c, sib_peer(k)).wait_recv())
-        w = jnp.dot(xt[...], grads[:, c].reshape(N_DP * ROWS, W_COL), preferred_element_type=F32)
-        wsend[c] = w.astype(BF16).reshape(N_X, W_X, W_COL)
-        loop(1, N_X, lambda k: copy8(c, x_peer(k), x, x_peer(k)).start())
-        xland[c, x] = wsend[c, x]
-
-    def sum_x(c):
-        loop(1, N_X, lambda k: copy8(c, x, x_peer(k), x_peer(k)).wait_recv())
-        acc = xland[c, 0].astype(F32)
-        for n in range(1, N_X):
-            acc += xland[c, n].astype(F32)
+        loop(0, LINE, lambda k: copy7(c, across(c % 2, k)).wait_recv())
+        xt = (xta, xtb)[c % 2][...].reshape(W_DP, N_DP * ROWS)
+        w = jnp.dot(xt, grads[c].reshape(N_DP * ROWS, W_COL), preferred_element_type=F32)
+        wsend[c] = w.astype(BF16).reshape(LINE, W_X, W_COL)
+        loop(1, LINE, lambda k: copy8(c, rest(c % 2, k)[0], place(c), k).start())
+        wland[c, place(c)] = wsend[c, place(c)]
+
+    def sum_line(c):
+        loop(1, LINE, lambda k: copy8(c, place(c), rest(c % 2, k)[0], k).wait_recv())
+        acc = wland[c, 0].astype(F32)
+        for n in range(1, LINE):
+            acc += wland[c, n].astype(F32)
         pad = jnp.zeros((PIECE - W_DEV, W_COL), F32)
         for n in range(N_Z):
             block = jnp.concatenate([acc[n * W_DEV : (n + 1) * W_DEV], pad], axis=0)
@@ -404,27 +469,40 @@
             acc += zland[c, n].astype(F32)
         out_ref[:, c * W_COL : (c + 1) * W_COL] = acc[:W_DEV]
 
+    loop(1, N_DP, lambda k: copy5(dp, dp_peer(k), dp_peer(k)).wait_recv())
+    loop(1, 2 * N_X, lambda k: copy0(team, team_peer(k), team_peer(k)).wait_recv())
+    loop(1, N_CTX, lambda k: copy4(0, me, ctx_peer(k), ctx_peer(k)).wait_recv())
+    assemble(0)
+    assemble(1)
     forward(0)
+    forward(1)
+    loop(1, N_CTX, lambda k: copy4(1, me, ctx_peer(k), ctx_peer(k)).wait_recv())
+    assemble(2)
+    assemble(3)
+    multiply(0)
+    multiply(1)
+    forward(2)
+    forward(3)
+    multiply(2)
+    multiply(3)
     for c in range(CHUNKS):
-        if c + 1 < CHUNKS:
-            forward(c + 1)
-        multiply(c)
-    for c in range(CHUNKS):
-        sum_x(c)
+        sum_line(c)
     for c in range(CHUNKS):
         sum_z(c)
 
     loop(1, N_CTX, lambda k: copy1(ctx_peer(k), me, ctx_peer(k)).wait_send())
     loop(1, N_DP, lambda k: copy5(dp_peer(k), dp, dp_peer(k)).wait_send())
+    loop(1, 2 * N_X, lambda k: copy0(team_peer(k), team, team_peer(k)).wait_send())
     for s in range(2):
         loop(1, N_PIECE, lambda k, s=s: copy2(s, k, reader(k), piece_here).wait_send())
         loop(1, N_PIECE, lambda k, s=s: copy3(s, k, piece_of(holder(k)), me, holder(k)).wait_send())
     for kind in range(2):
         loop(1, N_CTX, lambda k, kind=kind: copy4(kind, ctx_peer(k), me, ctx_peer(k)).wait_send())
     for c in range(CHUNKS):
-        loop(1, 4, lambda k, c=c: copy6(c, dp, y_peer(k)).wait_send())
-        loop(0, 4, lambda k, c=c: copy7(c, y_peer(k)).wait_send())
-        loop(1, N_X, lambda k, c=c: copy8(c, x_peer(k), x, x_peer(k)).wait_send())
+        loop(1, LINE, lambda k, c=c: copy6(c, member(c), k).wait_send())
+        copy7(c, member(c)).wait_send()
+        loop(1, LINE, lambda k, c=c: copy7(c, line(c % 2, k)[0]).wait_send())
+        loop(1, LINE, lambda k, c=c: copy8(c, rest(c % 2, k)[0], place(c), k).wait_send())
         loop(1, N_Z, lambda k, c=c: copy9(c, z_peer(k), z, z_peer(k)).wait_send())
     dq_copy.wait()
 
@@ -455,8 +533,9 @@
             vmem((ROWS, KVC), BF16),
             vmem((ROWS, KVC), BF16),
             vmem((ROWS, wide), BF16),
-            vmem((ROWS, HD), F32),
-            vmem((ROWS, HD), F32),
+            vmem((ROWS, DW), BF16),
+            vmem((2, KEYS, HD), F32),
+            vmem((2, KEYS, HD), F32),
             vmem((2, KEYS, HD), F32),
             vmem((ROWS, wide), BF16),
             vmem((ROWS, wide), BF16),
@@ -469,9 +548,10 @@
             vmem((N_CTX * REACH + 1, 2) + tile, BF16),
             vmem((2, N_CTX, 2) + tile, BF16),
             vmem((2, N_CTX, 2) + tile, BF16),
-            vmem((N_DP, ROWS, W_DP), BF16),
-            vmem((W_DP, N_DP * ROWS), BF16),
-            vmem((N_DP, CHUNKS, ROWS, W_COL), BF16),
+            vmem((N_Y, 2, N_X, W_X, ROWS), BF16),
+            vmem((N_X, W_X, N_DP * ROWS), BF16),
+            vmem((N_Y, W_X, N_DP * ROWS), BF16),
+            vmem((CHUNKS, N_DP, ROWS, W_COL), BF16),
             vmem((CHUNKS, N_X, W_X, W_COL), BF16),
             vmem((CHUNKS, N_X, W_X, W_COL), BF16),
             vmem((CHUNKS, N_Z, PIECE, W_COL), BF16),
@@ -482,7 +562,8 @@
             dma((2, N_PIECE)), dma((2, N_PIECE)),
             dma((2, N_CTX)), dma((2, N_CTX)),
             dma((N_DP,)), dma((N_DP,)),
-            dma((CHUNKS, N_DP)), dma((CHUNKS, N_DP)),
+            dma((N_DP,)), dma((N_DP,)),
+            dma((CHUNKS, LINE)), dma((CHUNKS, N_DP)),
             dma((CHUNKS, N_DP)), dma((CHUNKS, N_DP)),
             dma((CHUNKS, N_X)), dma((CHUNKS, N_X)),
             dma((CHUNKS, N_Z)), dma((CHUNKS, N_Z)),

time: 100 us -> 104 us (1.040)
  Pallas kernels: 96.7 us -> 99.8 us
    pallas_call x1, Pallas kernels: 96.7 us -> 99.8 us  [per_device(): pl.pallas_call(kernel, out_shape=[jax.ShapeDtypeStruct((ROWS, wide), BF16...]
where the time goes in v3:
time: 104 us; the launch traced here: 103 us
  Pallas kernels  99.8 us (96%)
  local copies, waits for them, and re-layouts  2.95 us (3%)
    pallas_call x1, Pallas kernels, per_device(): pl.pallas_call(kernel, out_shape=[jax.ShapeDtypeStruct((ROWS, wide), BF16...  99.8 us
    unnamed x4, local copies, waits for them, and re-layouts  2.95 us

profile of v3, /device:TPU:1, one launch (start us, length us, event | category | flops | bytes accessed | tf_op | source)
XLA Modules:
  0.0 103.5 jit_solution(17785516740972987134)
XLA Ops:
  0.6 99.8 %packed_backward.1 = (bf16[128,4096]{1,0:T(8,128)(2,1)}, f32[12,1024]{1,0:T(8,128)}) custom-call(s32[1,64]{1,0:T(1,128)} %span_h.1, s32[1,32]{1,0:T(1,128)} %len_h.1, f32[1,128]{1,0:T(1,128)} %constant.4.clone.freq_h, bf16[384,384]{1,0:T(8,128)(2,1)} %constant.5.clone.perm_h, bf16[128,4096]{1,0:T(8,128)(2,1)} %q_h.1, bf16[128,512]{1,0:T(8,128)(2,1)} %k_h.1, ...), custom_call_target="tpu_custom_call" | custom-call | tf_op jit(solution)/shard_map/packed_backward/pallas_call | solution.py:515
  100.5 0.0 copy-start
  100.5 2.3 %copy.13 = bf16[128,4096]{1,0:T(8,128)(2,1)} copy(bf16[128,4096]{1,0:T(8,128)(2,1)} %get-tuple-element.4) | data formatting | bytes 2097152
  102.8 0.0 copy-done
  102.8 0.6 copy.14
Async XLA Ops:
  100.5 2.3 %copy-start = (f32[12,1024]{1,0:T(8,128)S(1)}, f32[12,1024]{1,0:T(8,128)}, u32[]{:S(2)}) copy-start(f32[12,1024]{1,0:T(8,128)} %get-tuple-element.5) | copy-start | bytes 147460

commit v4 on v3

--- a/solution.py
+++ b/solution.py
@@ -106,6 +106,10 @@
         sin[n * rows : (n + 1) * rows] = jnp.where(lane < half, -s0, jnp.where(lane < ROT, s1, 0.0))
 
 
+def settle(ref, sem):
+    pltpu.make_async_copy(ref, ref, sem).wait()
+
+
 def lanes(at, size):
     return pl.ds(pl.multiple_of(at, HD), size)
 
@@ -114,7 +118,7 @@
     span_h, len_h, freq_h, perm_h, q_h, k_h, v_h, do_h, in_h, dq_h, out_ref,
     span, lens, slot_of, take, give,
     slot_v, freq, perm, q, keys, vals, do, feats, cos, sin, bias, qrot, dq,
-    pack, held, chosen, win, part, own, landed, total, back, turned, xta, xtb,
+    pack, held, chosen, win, part, own, kept_k, kept_ds, landed, total, back, turned, xta, xtb,
     grads, wsend, wland, zsend, zland,
     local, send1, recv1, send2, recv2, send3, recv3, send4, recv4, send5, recv5, send0, recv0,
     send6, recv6, send7, recv7, send8, recv8, send9, recv9,
@@ -123,11 +127,10 @@
     z, x = me // N_X, lax.rem(me, N_X)
     y, core = dp // 2, lax.rem(dp, 2)
     sib = dp + 1 - 2 * core
-    team = 2 * x + core
+    team = core * N_X + x
     ctx_peer = lambda k: lax.rem(me + k, N_CTX)
     dp_peer = lambda k: lax.rem(dp + k, N_DP)
     y_peer = lambda k: lax.rem(dp + 2 * k, N_DP)
-    sib_peer = lambda k: lax.rem(sib + 2 * k, N_DP)
     x_peer = lambda k: lax.rem(x + k, N_X)
     team_peer = lambda k: lax.rem(team + k, 2 * N_X)
     z_peer = lambda k: lax.rem(z + k, N_Z)
@@ -179,29 +182,28 @@
 
     def copy1(src, owner, peer):
         return remote(
-            pack.at[piece_of(src)], held.at[pl.ds(2 * owner, 2)], send1.at[src], recv1.at[owner], (dp, peer)
+            pack.at[piece_of(src)], held.at[pl.ds(2 * owner, 2)], send1, recv1, (dp, peer)
         )
 
     loop(1, N_CTX, lambda k: copy1(ctx_peer(k), me, ctx_peer(k)).start())
     held[pl.ds(2 * me, 2)] = pack[piece_here]
 
-    def copy5(src, owner, peer):
+    def copy5(peer):
         return remote(
-            turned.at[src // 2, lax.rem(src, 2)],
-            xta.at[:, :, lanes(owner * ROWS, ROWS)],
-            send5.at[src],
-            recv5.at[owner],
+            turned.at[peer // 2, lax.rem(peer, 2)],
+            xta.at[:, :, lanes((core * N_Y + y) * ROWS, ROWS)],
+            send5,
+            recv5,
             (peer, me),
         )
 
-    def copy0(src, owner, peer):
-        device = (dp - core + lax.rem(peer, 2), z * N_X + peer // 2)
+    def copy0(peer):
         return remote(
-            turned.at[:, lax.rem(src, 2), src // 2],
-            xtb.at[:, :, lanes(owner * ROWS, ROWS)],
-            send0.at[src],
-            recv0.at[owner],
-            device,
+            turned.at[:, peer // N_X, lax.rem(peer, N_X)],
+            xtb.at[:, :, lanes(team * ROWS, ROWS)],
+            send0,
+            recv0,
+            (dp - core + peer // N_X, z * N_X + lax.rem(peer, N_X)),
         )
 
     fetches[5].wait()
@@ -209,9 +211,9 @@
     for d in range(N_DP):
         w = lax.dot_general(perm[...], feats[:, d * W_DP : (d + 1) * W_DP], NT, preferred_element_type=F32)
         turned[d // 2, d % 2] = w.astype(BF16).reshape(N_X, W_X, ROWS)
-    loop(1, N_DP, lambda k: copy5(dp_peer(k), dp, dp_peer(k)).start())
-    loop(1, 2 * N_X, lambda k: copy0(team_peer(k), team, team_peer(k)).start())
-    xta[:, :, lanes(dp * ROWS, ROWS)] = turned[y, core]
+    loop(1, N_DP, lambda k: copy5(dp_peer(k)).start())
+    loop(1, 2 * N_X, lambda k: copy0(team_peer(k)).start())
+    xta[:, :, lanes((core * N_Y + y) * ROWS, ROWS)] = turned[y, core]
     xtb[:, :, lanes(team * ROWS, ROWS)] = turned[:, core, x]
 
     for copy in fetches[2:5]:
@@ -276,7 +278,7 @@
     loop(0, 2, lambda k: clear(2, 2 * k + 1))
     loop(0, 2, lambda k: clear(6, 2 * k))
     landed[N_CTX * REACH] = jnp.zeros((2, PIECE, HD), BF16)
-    loop(1, N_CTX, lambda k: copy1(me, ctx_peer(k), ctx_peer(k)).wait_recv())
+    settle(held.at[pl.ds(0, 2 * (N_CTX - 1))], recv1)
 
     def choose(s, k):
         device = reader(k)
@@ -284,7 +286,7 @@
             chosen[s, k, w] = held[take[device * REACH + s * BACK + w]]
 
     def copy2(s, k, peer, piece):
-        return remote(chosen.at[s, k], win.at[s, piece], send2.at[s, k], recv2.at[s, k], (dp, peer))
+        return remote(chosen.at[s, k], win.at[s, piece], send2, recv2.at[s], (dp, peer))
 
     for s in range(2):
 
@@ -301,13 +303,13 @@
         return remote(
             part.at[s, src],
             landed.at[pl.ds(REACH * owner + BACK * s, BACK)],
-            send3.at[s, k],
-            recv3.at[s, k],
+            send3,
+            recv3,
             (dp, peer),
         )
 
     for s in range(2):
-        loop(1, N_PIECE, lambda k, s=s: copy2(s, k, holder(k), piece_of(holder(k))).wait_recv())
+        settle(win.at[s, pl.ds(0, N_PIECE - 1)], recv2.at[s])
         rows = slice(s * SPAN, (s + 1) * SPAN)
 
         def attend(n, s=s, rows=rows):
@@ -351,23 +353,30 @@
                     copy3(s, at, piece_of(holder(at)), me, holder(at)).start()
 
             loop(0, N_ROW, hand_over)
-            dqt = lax.dot_general(k, dscores, TN, preferred_element_type=F32)
-            upright = dqt.T * SCALE
+            kept_k[s, j] = k
+            kept_ds[s, j] = dscores
+
+        loop(0, KVH, attend)
+        landed[pl.ds(REACH * me + BACK * s, BACK)] = part[s, piece_here]
+
+    def query_grads(j):
+        for s in range(2):
+            rows = slice(s * SPAN, (s + 1) * SPAN)
+            across_keys = lax.dot_general(kept_k[s, j], kept_ds[s, j], TN, preferred_element_type=F32)
+            upright = across_keys.T * SCALE
             for g in range(G):
                 u = upright[g * SPAN : (g + 1) * SPAN]
                 u = u * cos[s, BACK * SPAN :] - swap_halves(u) * sin[s, BACK * SPAN :]
                 dq[rows, lanes((j * G + g) * HD, HD)] = u.astype(BF16)
 
-        loop(0, KVH, attend)
-        landed[pl.ds(REACH * me + BACK * s, BACK)] = part[s, piece_here]
+    loop(0, KVH, query_grads)
     dq_copy = pltpu.make_async_copy(dq, dq_h, local.at[10])
     dq_copy.start()
-    for s in range(2):
-        loop(1, N_PIECE, lambda k, s=s: copy3(s, k, piece_here, reader(k), reader(k)).wait_recv())
+    settle(landed.at[pl.ds(0, REACH * (N_PIECE - 1))], recv3)
 
     def copy4(kind, src, owner, peer):
         return remote(
-            total.at[kind, src], back.at[kind, owner], send4.at[kind, src], recv4.at[kind, owner], (dp, peer)
+            total.at[kind, src], back.at[kind, owner], send4, recv4.at[kind], (dp, peer)
         )
 
     def sum_up(kind, device):
@@ -389,21 +398,17 @@
         back[kind, me] = total[kind, me]
 
     def line(half, k):
-        if half == 0:
-            return y_peer(k), (y_peer(k), me)
-        return 2 * x_peer(k) + core, (dp, z * N_X + x_peer(k))
-
-    def across(half, k):
-        return sib_peer(k) if half == 0 else 2 * x_peer(k) + 1 - core
-
-    def copy6(c, owner, k):
-        _, device = line(c % 2, k)
-        return remote(grads.at[c, owner], grads.at[c, owner], send6.at[c, k], recv6.at[c, owner], device)
-
-    def copy7(c, owner):
-        return remote(grads.at[c, owner], grads.at[c, owner], send7.at[c, owner], recv7.at[c, owner], (sib, me))
-
-    member = lambda c: (dp, team)[c % 2]
+        return (y_peer(k), me) if half == 0 else (dp, z * N_X + x_peer(k))
+
+    place = lambda c: (y, x)[c % 2]
+    far_place = lambda c: (x, y)[c % 2]
+
+    def copy6(c, k):
+        mine = grads.at[c, core, place(c)]
+        return remote(mine, mine, send6, recv6.at[c], line(c % 2, k))
+
+    def copy7(c):
+        return remote(grads.at[c, core], grads.at[c, core], send7, recv7.at[c], (sib, me))
 
     def assemble(c):
         kind, half = c // 2, c % 2
@@ -418,40 +423,35 @@
                     if kind == 0:
                         at = slice(BACK * SPAN + r * PIECE, BACK * SPAN + (r + 1) * PIECE)
                         g = g * cos[s, at] - swap_halves(g) * sin[s, at]
-                    grads[c, member(c), rows, n * HD : (n + 1) * HD] = g.astype(BF16)
-        loop(1, LINE, lambda k: copy6(c, member(c), k).start())
-        copy7(c, member(c)).start()
+                    grads[c, core, place(c), rows, n * HD : (n + 1) * HD] = g.astype(BF16)
+        loop(1, LINE, lambda k: copy6(c, k).start())
 
     def forward(c):
-        for k in range(1, LINE):
-            owner, _ = line(c % 2, k)
-            copy6(c, owner, k).wait_recv()
-            copy7(c, owner).start()
+        settle(grads.at[c, 0, pl.ds(0, LINE - 1)], recv6.at[c])
+        copy7(c).start()
 
     def rest(half, k):
         if half == 0:
             return x_peer(k), (dp, z * N_X + x_peer(k))
         return y_peer(k) // 2, (y_peer(k), me)
 
-    place = lambda c: (x, y)[c % 2]
-
-    def copy8(c, src, owner, k):
-        _, device = rest(c % 2, k)
-        return remote(wsend.at[c, src], wland.at[c, owner], send8.at[c, src], recv8.at[c, owner], device)
-
-    def copy9(c, src, owner, peer):
-        return remote(zsend.at[c, src], zland.at[c, owner], send9.at[c, src], recv9.at[c, owner], (dp, peer * N_X + x))
+    def copy8(c, k):
+        src, device = rest(c % 2, k)
+        return remote(wsend.at[c, src], wland.at[c, far_place(c)], send8, recv8.at[c], device)
+
+    def copy9(c, peer):
+        return remote(zsend.at[c, peer], zland.at[c, z], send9, recv9.at[c], (dp, peer * N_X + x))
 
     def multiply(c):
-        loop(0, LINE, lambda k: copy7(c, across(c % 2, k)).wait_recv())
+        settle(grads.at[c, 0], recv7.at[c])
         xt = (xta, xtb)[c % 2][...].reshape(W_DP, N_DP * ROWS)
         w = jnp.dot(xt, grads[c].reshape(N_DP * ROWS, W_COL), preferred_element_type=F32)
         wsend[c] = w.astype(BF16).reshape(LINE, W_X, W_COL)
-        loop(1, LINE, lambda k: copy8(c, rest(c % 2, k)[0], place(c), k).start())
-        wland[c, place(c)] = wsend[c, place(c)]
+        loop(1, LINE, lambda k: copy8(c, k).start())
+        wland[c, far_place(c)] = wsend[c, far_place(c)]
 
     def sum_line(c):
-        loop(1, LINE, lambda k: copy8(c, place(c), rest(c % 2, k)[0], k).wait_recv())
+        settle(wland.at[c, pl.ds(0, LINE - 1)], recv8.at[c])
         acc = wland[c, 0].astype(F32)
         for n in range(1, LINE):
             acc += wland[c, n].astype(F32)
@@ -459,26 +459,26 @@
         for n in range(N_Z):
             block = jnp.concatenate([acc[n * W_DEV : (n + 1) * W_DEV], pad], axis=0)
             zsend[c, n] = block.astype(BF16)
-        loop(1, N_Z, lambda k: copy9(c, z_peer(k), z, z_peer(k)).start())
+        loop(1, N_Z, lambda k: copy9(c, z_peer(k)).start())
         zland[c, z] = zsend[c, z]
 
     def sum_z(c):
-        loop(1, N_Z, lambda k: copy9(c, z, z_peer(k), z_peer(k)).wait_recv())
+        settle(zland.at[c, pl.ds(0, N_Z - 1)], recv9.at[c])
         acc = zland[c, 0].astype(F32)
         for n in range(1, N_Z):
             acc += zland[c, n].astype(F32)
         out_ref[:, c * W_COL : (c + 1) * W_COL] = acc[:W_DEV]
 
-    loop(1, N_DP, lambda k: copy5(dp, dp_peer(k), dp_peer(k)).wait_recv())
-    loop(1, 2 * N_X, lambda k: copy0(team, team_peer(k), team_peer(k)).wait_recv())
-    loop(1, N_CTX, lambda k: copy4(0, me, ctx_peer(k), ctx_peer(k)).wait_recv())
+    settle(xta.at[:, :, pl.ds(0, (N_DP - 1) * ROWS)], recv5)
+    settle(xtb.at[:, :, pl.ds(0, (N_DP - 1) * ROWS)], recv0)
+    settle(back.at[0, pl.ds(0, N_CTX - 1)], recv4.at[0])
     assemble(0)
     assemble(1)
+    settle(back.at[1, pl.ds(0, N_CTX - 1)], recv4.at[1])
+    assemble(2)
+    assemble(3)
     forward(0)
     forward(1)
-    loop(1, N_CTX, lambda k: copy4(1, me, ctx_peer(k), ctx_peer(k)).wait_recv())
-    assemble(2)
-    assemble(3)
     multiply(0)
     multiply(1)
     forward(2)
@@ -490,20 +490,16 @@
     for c in range(CHUNKS):
         sum_z(c)
 
-    loop(1, N_CTX, lambda k: copy1(ctx_peer(k), me, ctx_peer(k)).wait_send())
-    loop(1, N_DP, lambda k: copy5(dp_peer(k), dp, dp_peer(k)).wait_send())
-    loop(1, 2 * N_X, lambda k: copy0(team_peer(k), team, team_peer(k)).wait_send())
-    for s in range(2):
-        loop(1, N_PIECE, lambda k, s=s: copy2(s, k, reader(k), piece_here).wait_send())
-        loop(1, N_PIECE, lambda k, s=s: copy3(s, k, piece_of(holder(k)), me, holder(k)).wait_send())
-    for kind in range(2):
-        loop(1, N_CTX, lambda k, kind=kind: copy4(kind, ctx_peer(k), me, ctx_peer(k)).wait_send())
-    for c in range(CHUNKS):
-        loop(1, LINE, lambda k, c=c: copy6(c, member(c), k).wait_send())
-        copy7(c, member(c)).wait_send()
-        loop(1, LINE, lambda k, c=c: copy7(c, line(c % 2, k)[0]).wait_send())
-        loop(1, LINE, lambda k, c=c: copy8(c, rest(c % 2, k)[0], place(c), k).wait_send())
-        loop(1, N_Z, lambda k, c=c: copy9(c, z_peer(k), z, z_peer(k)).wait_send())
+    settle(held.at[pl.ds(0, 2 * (N_CTX - 1))], send1)
+    settle(xta.at[:, :, pl.ds(0, (N_DP - 1) * ROWS)], send5)
+    settle(xtb.at[:, :, pl.ds(0, (N_DP - 1) * ROWS)], send0)
+    settle(chosen.at[:, pl.ds(0, N_PIECE - 1)], send2)
+    settle(part.at[:, pl.ds(0, N_PIECE - 1)], send3)
+    settle(total.at[:, pl.ds(0, N_CTX - 1)], send4)
+    settle(grads.at[:, 0, pl.ds(0, LINE - 1)], send6)
+    settle(grads.at[:, 0], send7)
+    settle(wsend.at[:, pl.ds(0, LINE - 1)], send8)
+    settle(zsend.at[:, pl.ds(0, N_Z - 1)], send9)
     dq_copy.wait()
 
 
@@ -545,28 +541,30 @@
             vmem((2, N_PIECE, BACK, 2) + tile, BF16),
             vmem((2, N_PIECE, BACK, 2) + tile, BF16),
             vmem((2, ROWS, KVC), F32),
+            vmem((2, KVH, KEYS, HD), BF16),
+            vmem((2, KVH, KEYS, G * SPAN), BF16),
             vmem((N_CTX * REACH + 1, 2) + tile, BF16),
             vmem((2, N_CTX, 2) + tile, BF16),
             vmem((2, N_CTX, 2) + tile, BF16),
             vmem((N_Y, 2, N_X, W_X, ROWS), BF16),
             vmem((N_X, W_X, N_DP * ROWS), BF16),
             vmem((N_Y, W_X, N_DP * ROWS), BF16),
-            vmem((CHUNKS, N_DP, ROWS, W_COL), BF16),
+            vmem((CHUNKS, 2, LINE, ROWS, W_COL), BF16),
             vmem((CHUNKS, N_X, W_X, W_COL), BF16),
             vmem((CHUNKS, N_X, W_X, W_COL), BF16),
             vmem((CHUNKS, N_Z, PIECE, W_COL), BF16),
             vmem((CHUNKS, N_Z, PIECE, W_COL), BF16),
             dma((11,)),
-            dma((N_CTX,)), dma((N_CTX,)),
-            dma((2, N_PIECE)), dma((2, N_PIECE)),
-            dma((2, N_PIECE)), dma((2, N_PIECE)),
-            dma((2, N_CTX)), dma((2, N_CTX)),
-            dma((N_DP,)), dma((N_DP,)),
-            dma((N_DP,)), dma((N_DP,)),
-            dma((CHUNKS, LINE)), dma((CHUNKS, N_DP)),
-            dma((CHUNKS, N_DP)), dma((CHUNKS, N_DP)),
-            dma((CHUNKS, N_X)), dma((CHUNKS, N_X)),
-            dma((CHUNKS, N_Z)), dma((CHUNKS, N_Z)),
+            dma, dma,
+            dma, dma((2,)),
+            dma, dma,
+            dma, dma((2,)),
+            dma, dma,
+            dma, dma,
+            dma, dma((CHUNKS,)),
+            dma, dma((CHUNKS,)),
+            dma, dma((CHUNKS,)),
+            dma, dma((CHUNKS,)),
         ],
         compiler_params=pltpu.CompilerParams(
             collective_id=0, has_side_effects=True, vmem_limit_bytes=VMEM_LIMIT

time: 104 us -> 91.4 us (0.88)
  Pallas kernels: 99.8 us -> 87.7 us
    pallas_call x1, Pallas kernels: 99.8 us -> 87.7 us  [per_device(): pl.pallas_call(kernel, out_shape=[jax.ShapeDtypeStruct((ROWS, wide), BF16...]
where the time goes in v4:
time: 91.4 us; the launch traced here: 91.3 us
  Pallas kernels  87.7 us (96%)
  local copies, waits for them, and re-layouts  2.95 us (3%)
    pallas_call x1, Pallas kernels, per_device(): pl.pallas_call(kernel, out_shape=[jax.ShapeDtypeStruct((ROWS, wide), BF16...  87.7 us
    unnamed x4, local copies, waits for them, and re-layouts  2.95 us

profile of v4, /device:TPU:1, one launch (start us, length us, event | category | flops | bytes accessed | tf_op | source)
XLA Modules:
  0.0 91.3 jit_solution(2636225341325046632)
XLA Ops:
  0.6 87.7 %packed_backward.1 = (bf16[128,4096]{1,0:T(8,128)(2,1)}, f32[12,1024]{1,0:T(8,128)}) custom-call(s32[1,64]{1,0:T(1,128)} %span_h.1, s32[1,32]{1,0:T(1,128)} %len_h.1, f32[1,128]{1,0:T(1,128)} %constant.4.clone.freq_h, bf16[384,384]{1,0:T(8,128)(2,1)} %constant.5.clone.perm_h, bf16[128,4096]{1,0:T(8,128)(2,1)} %q_h.1, bf16[128,512]{1,0:T(8,128)(2,1)} %k_h.1, ...), custom_call_target="tpu_custom_call" | custom-call | tf_op jit(solution)/shard_map/packed_backward/pallas_call | solution.py:511
  88.3 0.0 copy-start
  88.4 2.3 %copy.13 = bf16[128,4096]{1,0:T(8,128)(2,1)} copy(bf16[128,4096]{1,0:T(8,128)(2,1)} %get-tuple-element.4) | data formatting | bytes 2097152
  90.7 0.0 copy-done
  90.7 0.6 copy.14
Async XLA Ops:
  88.3 2.3 %copy-start = (f32[12,1024]{1,0:T(8,128)S(1)}, f32[12,1024]{1,0:T(8,128)}, u32[]{:S(2)}) copy-start(f32[12,1024]{1,0:T(8,128)} %get-tuple-element.5) | copy-start | bytes 147460

commit v5 on v4

--- a/solution.py
+++ b/solution.py
@@ -38,6 +38,7 @@
 W_DEV = W_DP // N_CTX
 W_X = W_DP // N_X
 CHUNKS = 4
+HEADS = 2 * KVH // CHUNKS
 W_COL = 2 * KVC // CHUNKS
 N_Y = N_DP // 2
 LINE = 4
@@ -118,21 +119,24 @@
     span_h, len_h, freq_h, perm_h, q_h, k_h, v_h, do_h, in_h, dq_h, out_ref,
     span, lens, slot_of, take, give,
     slot_v, freq, perm, q, keys, vals, do, feats, cos, sin, bias, qrot, dq,
-    pack, held, chosen, win, part, own, kept_k, kept_ds, landed, total, back, turned, xta, xtb,
+    pack, held_k, held_v, chosen, win, part, own, kept_k, kept_ds, landed_k, landed_v, total, back, turned, xt,
     grads, wsend, wland, zsend, zland,
-    local, send1, recv1, send2, recv2, send3, recv3, send4, recv4, send5, recv5, send0, recv0,
+    local, send1, recv1, send2, recv2, send3, recv3, send4, recv4, send5, recv5,
     send6, recv6, send7, recv7, send8, recv8, send9, recv9,
 ):
     dp, me = lax.axis_index("dp"), lax.axis_index("ctx")
     z, x = me // N_X, lax.rem(me, N_X)
     y, core = dp // 2, lax.rem(dp, 2)
     sib = dp + 1 - 2 * core
-    team = core * N_X + x
     ctx_peer = lambda k: lax.rem(me + k, N_CTX)
+    def far_peer(k):
+        n = N_CTX - 1 - k
+        step = n // 2 + 1
+        return ctx_peer(jnp.where(lax.rem(n, 2) == 0, step, N_CTX - step))
+
     dp_peer = lambda k: lax.rem(dp + k, N_DP)
     y_peer = lambda k: lax.rem(dp + 2 * k, N_DP)
     x_peer = lambda k: lax.rem(x + k, N_X)
-    team_peer = lambda k: lax.rem(team + k, 2 * N_X)
     z_peer = lambda k: lax.rem(z + k, N_Z)
     piece_here = lax.rem(z, N_ROW) * KVH + x
 
@@ -151,6 +155,8 @@
 
     def piece_of(device):
         return lax.rem(device, N_PIECE)
+
+    held, landed = (held_k, held_v), (landed_k, landed_v)
 
     fetches = [
         pltpu.make_async_copy(src, dst, local.at[n])
@@ -168,7 +174,6 @@
 
     loop(1, N_CTX, lambda k: greet((dp, ctx_peer(k))))
     loop(1, N_DP, lambda k: greet((dp_peer(k), me)))
-    loop(1, N_X, lambda k: greet((sib, z * N_X + x_peer(k))))
     for copy in fetches[:2]:
         copy.wait()
     for s in range(2):
@@ -176,45 +181,37 @@
             rows = slice(s * SPAN + r * PIECE, s * SPAN + (r + 1) * PIECE)
             for j in range(KVH):
                 cols = slice(j * HD, (j + 1) * HD)
-                pack[r * KVH + j, s, 0] = keys[rows, cols]
-                pack[r * KVH + j, s, 1] = vals[rows, cols]
-    pl.semaphore_wait(barrier, N_CTX - 1 + N_DP - 1 + N_X - 1)
-
-    def copy1(src, owner, peer):
+                pack[0, r * KVH + j, s] = keys[rows, cols]
+                pack[1, r * KVH + j, s] = vals[rows, cols]
+    pl.semaphore_wait(barrier, N_CTX - 1 + N_DP - 1)
+
+    def copy1(kind, peer):
         return remote(
-            pack.at[piece_of(src)], held.at[pl.ds(2 * owner, 2)], send1, recv1, (dp, peer)
+            pack.at[kind, piece_of(peer)], held[kind].at[pl.ds(2 * me, 2)], send1.at[kind], recv1.at[kind], (dp, peer)
         )
 
-    loop(1, N_CTX, lambda k: copy1(ctx_peer(k), me, ctx_peer(k)).start())
-    held[pl.ds(2 * me, 2)] = pack[piece_here]
+    def spread(kind):
+        loop(1, N_CTX, lambda k: copy1(kind, far_peer(k)).start())
+        held[kind][pl.ds(2 * me, 2)] = pack[kind, piece_here]
+
+    spread(0)
 
     def copy5(peer):
         return remote(
-            turned.at[peer // 2, lax.rem(peer, 2)],
-            xta.at[:, :, lanes((core * N_Y + y) * ROWS, ROWS)],
+            turned.at[peer],
+            xt.at[:, lanes((core * N_Y + y) * ROWS, ROWS)],
             send5,
             recv5,
             (peer, me),
         )
 
-    def copy0(peer):
-        return remote(
-            turned.at[:, peer // N_X, lax.rem(peer, N_X)],
-            xtb.at[:, :, lanes(team * ROWS, ROWS)],
-            send0,
-            recv0,
-            (dp - core + peer // N_X, z * N_X + lax.rem(peer, N_X)),
-        )
-
     fetches[5].wait()
     fetches[6].wait()
     for d in range(N_DP):
         w = lax.dot_general(perm[...], feats[:, d * W_DP : (d + 1) * W_DP], NT, preferred_element_type=F32)
-        turned[d // 2, d % 2] = w.astype(BF16).reshape(N_X, W_X, ROWS)
+        turned[d] = w.astype(BF16)
     loop(1, N_DP, lambda k: copy5(dp_peer(k)).start())
-    loop(1, 2 * N_X, lambda k: copy0(team_peer(k)).start())
-    xta[:, :, lanes((core * N_Y + y) * ROWS, ROWS)] = turned[y, core]
-    xtb[:, :, lanes(team * ROWS, ROWS)] = turned[:, core, x]
+    xt[:, lanes((core * N_Y + y) * ROWS, ROWS)] = turned[dp]
 
     for copy in fetches[2:5]:
         copy.wait()
@@ -238,6 +235,8 @@
         at = pl.ds(0, BACK * SPAN)
         rope_tables(pos, lens, freq, cos.at[s, at], sin.at[s, at])
     slot_copy.wait()
+    settle(held[0].at[pl.ds(0, 2 * (N_CTX - 1))], send1.at[0])
+    spread(1)
 
     def fill(slot):
         at = span[0, slot]
@@ -268,65 +267,86 @@
             qrot[rows, lanes(h * HD, HD)] = v.astype(BF16)
 
     loop(0, KVH * G, rotate)
-    empty = jnp.zeros((REACH, 2, PIECE, HD), BF16)
+    empty = jnp.zeros((REACH, PIECE, HD), BF16)
 
     def clear(dz, dx):
         device = lax.rem(z + dz, N_Z) * N_X + lax.rem(x + dx, N_X)
-        landed[pl.ds(REACH * device, REACH)] = empty
+        for side in landed:
+            side[pl.ds(REACH * device, REACH)] = empty
 
     loop(0, 12, lambda k: clear(3 + k // N_X, lax.rem(k, N_X)))
     loop(0, 2, lambda k: clear(2, 2 * k + 1))
     loop(0, 2, lambda k: clear(6, 2 * k))
-    landed[N_CTX * REACH] = jnp.zeros((2, PIECE, HD), BF16)
-    settle(held.at[pl.ds(0, 2 * (N_CTX - 1))], recv1)
-
-    def choose(s, k):
+    for side in landed:
+        side[N_CTX * REACH] = jnp.zeros((PIECE, HD), BF16)
+
+    def choose(kind, s, k):
         device = reader(k)
         for w in range(BACK):
-            chosen[s, k, w] = held[take[device * REACH + s * BACK + w]]
-
-    def copy2(s, k, peer, piece):
-        return remote(chosen.at[s, k], win.at[s, piece], send2, recv2.at[s], (dp, peer))
+            chosen[kind, s, k, w] = held[kind][take[device * REACH + s * BACK + w]]
+
+    def copy2(kind, s, k):
+        return remote(
+            chosen.at[kind, s, k], win.at[kind, s, piece_here], send2, recv2.at[s], (dp, reader(k))
+        )
+
+    for kind in range(2):
+        settle(held[kind].at[pl.ds(0, 2 * (N_CTX - 1))], recv1.at[kind])
+        for s in range(2):
+
+            def serve(k, kind=kind, s=s):
+                k = 1 + lax.rem(k + 6, N_PIECE - 1)
+                choose(kind, s, k)
+                copy2(kind, s, k).start()
+
+            loop(1, N_PIECE, serve)
+            choose(kind, s, 0)
+            win[kind, s, piece_here] = chosen[kind, s, 0]
+    fetches[8].wait()
+
+    def copy3(kind, s, k):
+        return remote(
+            part.at[kind, s, piece_of(holder(k))],
+            landed[kind].at[pl.ds(REACH * me + BACK * s, BACK)],
+            send3,
+            recv3.at[kind],
+            (dp, holder(k)),
+        )
+
+    def hand_over(kind, s, n, grad):
+        j = lax.rem(x + n, KVH)
+        earlier = grad[: BACK * SPAN].astype(BF16).reshape(N_ROW, BACK, PIECE, HD)
+        for r in range(N_ROW):
+            part[kind, s, r * KVH + j] = earlier[r]
+        own[kind, s * SPAN : (s + 1) * SPAN, lanes(j * HD, HD)] = grad[BACK * SPAN :]
+
+        def send(dz):
+            at = dz * N_X + lax.rem(N_X - n, N_X)
+
+            @pl.when(at > 0)
+            def _():
+                copy3(kind, s, at).start()
+
+        loop(0, N_ROW, send)
+
+    def stacked(ref, s, j):
+        rows = slice(s * SPAN, (s + 1) * SPAN)
+        return jnp.concatenate([ref[rows, lanes((j * G + g) * HD, HD)] for g in range(G)], axis=0)
 
     for s in range(2):
-
-        def serve(k, s=s):
-            choose(s, k)
-            copy2(s, k, reader(k), piece_here).start()
-
-        loop(1, N_PIECE, serve)
-        choose(s, 0)
-        win[s, piece_here] = chosen[s, 0]
-    fetches[8].wait()
-
-    def copy3(s, k, src, owner, peer):
-        return remote(
-            part.at[s, src],
-            landed.at[pl.ds(REACH * owner + BACK * s, BACK)],
-            send3,
-            recv3,
-            (dp, peer),
-        )
-
-    for s in range(2):
-        settle(win.at[s, pl.ds(0, N_PIECE - 1)], recv2.at[s])
-        rows = slice(s * SPAN, (s + 1) * SPAN)
-
-        def attend(n, s=s, rows=rows):
+        settle(win.at[:, s, pl.ds(0, N_PIECE - 1)], recv2.at[s])
+
+        def attend(n, s=s):
             j = lax.rem(x + n, KVH)
 
             def window(kind):
-                parts = [win[s, r * KVH + j, :, kind].reshape(BACK * PIECE, HD) for r in range(N_ROW)]
-                parts += [pack[r * KVH + j, s, kind] for r in range(N_ROW)]
-                return jnp.concatenate(parts, axis=0)
-
-            def stacked(ref):
-                parts = [ref[rows, lanes((j * G + g) * HD, HD)] for g in range(G)]
+                parts = [win[kind, s, r * KVH + j].reshape(BACK * PIECE, HD) for r in range(N_ROW)]
+                parts += [pack[kind, r * KVH + j, s] for r in range(N_ROW)]
                 return jnp.concatenate(parts, axis=0)
 
             k, v = window(0).astype(F32), window(1)
             k = (k * cos[s] + swap_halves(k) * sin[s]).astype(BF16)
-            qs, dos = stacked(qrot), stacked(do)
+            qs, dos = stacked(qrot, s, j), stacked(do, s, j)
             mask = jnp.concatenate([bias[s]] * (G * SPAN // HD), axis=1)
             scores = lax.dot_general(k, qs, NT, preferred_element_type=F32)
             scores = scores * (SCALE * float(np.log2(np.e))) + mask
@@ -336,28 +356,19 @@
             delta = jnp.sum(probs * dprobs, axis=0, keepdims=True)
             dscores = (probs * (dprobs - delta)).astype(BF16)
             low = probs.astype(BF16)
-            dk = jnp.dot(dscores, qs, preferred_element_type=F32) * SCALE
-            dv = jnp.dot(low, dos, preferred_element_type=F32)
-            for kind, grad in ((0, dk), (1, dv)):
-                earlier = grad[: BACK * SPAN].astype(BF16).reshape(N_ROW, BACK, PIECE, HD)
-                for r in range(N_ROW):
-                    part[s, r * KVH + j, :, kind] = earlier[r]
-                own[kind, rows, lanes(j * HD, HD)] = grad[BACK * SPAN :]
-            dx = lax.rem(N_X - n, N_X)
-
-            def hand_over(dz):
-                at = dz * N_X + dx
-
-                @pl.when(at > 0)
-                def _():
-                    copy3(s, at, piece_of(holder(at)), me, holder(at)).start()
-
-            loop(0, N_ROW, hand_over)
+            hand_over(1, s, n, jnp.dot(low, dos, preferred_element_type=F32))
             kept_k[s, j] = k
             kept_ds[s, j] = dscores
 
+        def key_part(n, s=s):
+            j = lax.rem(x + n, KVH)
+            dk = jnp.dot(kept_ds[s, j], stacked(qrot, s, j), preferred_element_type=F32)
+            hand_over(0, s, n, dk * SCALE)
+
         loop(0, KVH, attend)
-        landed[pl.ds(REACH * me + BACK * s, BACK)] = part[s, piece_here]
+        loop(0, KVH, key_part)
+        for kind in range(2):
+            landed[kind][pl.ds(REACH * me + BACK * s, BACK)] = part[kind, s, piece_here]
 
     def query_grads(j):
         for s in range(2):
@@ -372,7 +383,6 @@
     loop(0, KVH, query_grads)
     dq_copy = pltpu.make_async_copy(dq, dq_h, local.at[10])
     dq_copy.start()
-    settle(landed.at[pl.ds(0, REACH * (N_PIECE - 1))], recv3)
 
     def copy4(kind, src, owner, peer):
         return remote(
@@ -382,38 +392,33 @@
     def sum_up(kind, device):
         for s in range(2):
             at = (2 * device + s) * BACK
-            acc = landed[give[at], kind].astype(F32)
+            acc = landed[kind][give[at]].astype(F32)
             for w in range(1, BACK):
-                acc += landed[give[at + w], kind].astype(F32)
+                acc += landed[kind][give[at + w]].astype(F32)
             total[kind, device, s] = acc.astype(BF16)
 
-    for kind in range(2):
+    for kind in (1, 0):
+        settle(landed[kind].at[pl.ds(0, REACH * (N_PIECE - 1))], recv3.at[kind])
 
         def give_back(k, kind=kind):
-            sum_up(kind, ctx_peer(k))
-            copy4(kind, ctx_peer(k), me, ctx_peer(k)).start()
+            sum_up(kind, far_peer(k))
+            copy4(kind, far_peer(k), me, far_peer(k)).start()
 
         loop(1, N_CTX, give_back)
         sum_up(kind, me)
         back[kind, me] = total[kind, me]
 
-    def line(half, k):
-        return (y_peer(k), me) if half == 0 else (dp, z * N_X + x_peer(k))
-
-    place = lambda c: (y, x)[c % 2]
-    far_place = lambda c: (x, y)[c % 2]
-
     def copy6(c, k):
-        mine = grads.at[c, core, place(c)]
-        return remote(mine, mine, send6, recv6.at[c], line(c % 2, k))
+        mine = grads.at[c, core, y]
+        return remote(mine, mine, send6, recv6.at[c], (y_peer(k), me))
 
     def copy7(c):
         return remote(grads.at[c, core], grads.at[c, core], send7, recv7.at[c], (sib, me))
 
     def assemble(c):
-        kind, half = c // 2, c % 2
-        for n in range(2):
-            j = 2 * half + n
+        kind = c * HEADS // KVH
+        for n in range(HEADS):
+            j = (c * HEADS + n) % KVH
             for r in range(N_ROW):
                 for s in range(2):
                     rows = slice(s * SPAN + r * PIECE, s * SPAN + (r + 1) * PIECE)
@@ -423,32 +428,26 @@
                     if kind == 0:
                         at = slice(BACK * SPAN + r * PIECE, BACK * SPAN + (r + 1) * PIECE)
                         g = g * cos[s, at] - swap_halves(g) * sin[s, at]
-                    grads[c, core, place(c), rows, n * HD : (n + 1) * HD] = g.astype(BF16)
+                    grads[c, core, y, rows, n * HD : (n + 1) * HD] = g.astype(BF16)
         loop(1, LINE, lambda k: copy6(c, k).start())
 
     def forward(c):
         settle(grads.at[c, 0, pl.ds(0, LINE - 1)], recv6.at[c])
         copy7(c).start()
 
-    def rest(half, k):
-        if half == 0:
-            return x_peer(k), (dp, z * N_X + x_peer(k))
-        return y_peer(k) // 2, (y_peer(k), me)
-
     def copy8(c, k):
-        src, device = rest(c % 2, k)
-        return remote(wsend.at[c, src], wland.at[c, far_place(c)], send8, recv8.at[c], device)
+        peer = x_peer(k)
+        return remote(wsend.at[c, peer], wland.at[c, x], send8, recv8.at[c], (dp, z * N_X + peer))
 
     def copy9(c, peer):
         return remote(zsend.at[c, peer], zland.at[c, z], send9, recv9.at[c], (dp, peer * N_X + x))
 
     def multiply(c):
         settle(grads.at[c, 0], recv7.at[c])
-        xt = (xta, xtb)[c % 2][...].reshape(W_DP, N_DP * ROWS)
-        w = jnp.dot(xt, grads[c].reshape(N_DP * ROWS, W_COL), preferred_element_type=F32)
+        w = jnp.dot(xt[...], grads[c].reshape(N_DP * ROWS, W_COL), preferred_element_type=F32)
         wsend[c] = w.astype(BF16).reshape(LINE, W_X, W_COL)
         loop(1, LINE, lambda k: copy8(c, k).start())
-        wland[c, far_place(c)] = wsend[c, far_place(c)]
+        wland[c, x] = wsend[c, x]
 
     def sum_line(c):
         settle(wland.at[c, pl.ds(0, LINE - 1)], recv8.at[c])
@@ -469,32 +468,28 @@
             acc += zland[c, n].astype(F32)
         out_ref[:, c * W_COL : (c + 1) * W_COL] = acc[:W_DEV]
 
-    settle(xta.at[:, :, pl.ds(0, (N_DP - 1) * ROWS)], recv5)
-    settle(xtb.at[:, :, pl.ds(0, (N_DP - 1) * ROWS)], recv0)
+    settle(xt.at[:, pl.ds(0, (N_DP - 1) * ROWS)], recv5)
+    settle(back.at[1, pl.ds(0, N_CTX - 1)], recv4.at[1])
+    values, keyed = range(CHUNKS // 2, CHUNKS), range(CHUNKS // 2)
+    for c in values:
+        assemble(c)
     settle(back.at[0, pl.ds(0, N_CTX - 1)], recv4.at[0])
-    assemble(0)
-    assemble(1)
-    settle(back.at[1, pl.ds(0, N_CTX - 1)], recv4.at[1])
-    assemble(2)
-    assemble(3)
-    forward(0)
-    forward(1)
-    multiply(0)
-    multiply(1)
-    forward(2)
-    forward(3)
-    multiply(2)
-    multiply(3)
-    for c in range(CHUNKS):
+    for c in keyed:
+        assemble(c)
+    for part_of in (values, keyed):
+        for c in part_of:
+            forward(c)
+        for c in part_of:
+            multiply(c)
+    for c in (*values, *keyed):
         sum_line(c)
-    for c in range(CHUNKS):
+    for c in (*values, *keyed):
         sum_z(c)
 
-    settle(held.at[pl.ds(0, 2 * (N_CTX - 1))], send1)
-    settle(xta.at[:, :, pl.ds(0, (N_DP - 1) * ROWS)], send5)
-    settle(xtb.at[:, :, pl.ds(0, (N_DP - 1) * ROWS)], send0)
-    settle(chosen.at[:, pl.ds(0, N_PIECE - 1)], send2)
-    settle(part.at[:, pl.ds(0, N_PIECE - 1)], send3)
+    settle(held[1].at[pl.ds(0, 2 * (N_CTX - 1))], send1.at[1])
+    settle(xt.at[:, pl.ds(0, (N_DP - 1) * ROWS)], send5)
+    settle(chosen.at[:, :, pl.ds(0, N_PIECE - 1)], send2)
+    settle(part.at[:, :, pl.ds(0, N_PIECE - 1)], send3)
     settle(total.at[:, pl.ds(0, N_CTX - 1)], send4)
     settle(grads.at[:, 0, pl.ds(0, LINE - 1)], send6)
     settle(grads.at[:, 0], send7)
@@ -535,31 +530,31 @@
             vmem((2, KEYS, HD), F32),
             vmem((ROWS, wide), BF16),
             vmem((ROWS, wide), BF16),
-            vmem((N_PIECE, 2, 2) + tile, BF16),
-            vmem((SLOTS, 2) + tile, BF16),
-            vmem((2, N_PIECE, BACK, 2) + tile, BF16),
-            vmem((2, N_PIECE, BACK, 2) + tile, BF16),
-            vmem((2, N_PIECE, BACK, 2) + tile, BF16),
+            vmem((2, N_PIECE, 2) + tile, BF16),
+            vmem((SLOTS,) + tile, BF16),
+            vmem((SLOTS,) + tile, BF16),
+            vmem((2, 2, N_PIECE, BACK) + tile, BF16),
+            vmem((2, 2, N_PIECE, BACK) + tile, BF16),
+            vmem((2, 2, N_PIECE, BACK) + tile, BF16),
             vmem((2, ROWS, KVC), F32),
             vmem((2, KVH, KEYS, HD), BF16),
             vmem((2, KVH, KEYS, G * SPAN), BF16),
-            vmem((N_CTX * REACH + 1, 2) + tile, BF16),
+            vmem((N_CTX * REACH + 1,) + tile, BF16),
+            vmem((N_CTX * REACH + 1,) + tile, BF16),
             vmem((2, N_CTX, 2) + tile, BF16),
             vmem((2, N_CTX, 2) + tile, BF16),
-            vmem((N_Y, 2, N_X, W_X, ROWS), BF16),
-            vmem((N_X, W_X, N_DP * ROWS), BF16),
-            vmem((N_Y, W_X, N_DP * ROWS), BF16),
+            vmem((N_DP, W_DP, ROWS), BF16),
+            vmem((W_DP, N_DP * ROWS), BF16),
             vmem((CHUNKS, 2, LINE, ROWS, W_COL), BF16),
             vmem((CHUNKS, N_X, W_X, W_COL), BF16),
             vmem((CHUNKS, N_X, W_X, W_COL), BF16),
             vmem((CHUNKS, N_Z, PIECE, W_COL), BF16),
             vmem((CHUNKS, N_Z, PIECE, W_COL), BF16),
             dma((11,)),
-            dma, dma,
+            dma((2,)), dma((2,)),
             dma, dma((2,)),
-            dma, dma,
             dma, dma((2,)),
-            dma, dma,
+            dma, dma((2,)),
             dma, dma,
             dma, dma((CHUNKS,)),
             dma, dma((CHUNKS,)),
@@ -575,7 +570,6 @@
         queries, keys, values, grad_out, inputs,
     )
 
-
 def solution(mesh):
     rows = P(("dp", "ctx"), None)
     return jax.shard_map(

time: 91.4 us -> 87.9 us (0.962)
  Pallas kernels: 87.7 us -> 84.2 us
    pallas_call x1, Pallas kernels: 87.7 us -> 84.2 us  [per_device(): pl.pallas_call(kernel, out_shape=[jax.ShapeDtypeStruct((ROWS, wide), BF16...]
where the time goes in v5:
time: 87.9 us; the launch traced here: 87.8 us
  Pallas kernels  84.2 us (96%)
  local copies, waits for them, and re-layouts  2.95 us (3%)
    pallas_call x1, Pallas kernels, per_device(): pl.pallas_call(kernel, out_shape=[jax.ShapeDtypeStruct((ROWS, wide), BF16...  84.2 us
    unnamed x4, local copies, waits for them, and re-layouts  2.95 us

profile of v5, /device:TPU:1, one launch (start us, length us, event | category | flops | bytes accessed | tf_op | source)
XLA Modules:
  0.0 87.8 jit_solution(17652874067431611038)
XLA Ops:
  0.6 84.2 %packed_backward.1 = (bf16[128,4096]{1,0:T(8,128)(2,1)}, f32[12,1024]{1,0:T(8,128)}) custom-call(s32[1,64]{1,0:T(1,128)} %span_h.1, s32[1,32]{1,0:T(1,128)} %len_h.1, f32[1,128]{1,0:T(1,128)} %constant.4.clone.freq_h, bf16[384,384]{1,0:T(8,128)(2,1)} %constant.5.clone.perm_h, bf16[128,4096]{1,0:T(8,128)(2,1)} %q_h.1, bf16[128,512]{1,0:T(8,128)(2,1)} %k_h.1, ...), custom_call_target="tpu_custom_call" | custom-call | tf_op jit(solution)/shard_map/packed_backward/pallas_call | solution.py:506
  84.9 0.0 copy-start
  84.9 2.3 %copy.13 = bf16[128,4096]{1,0:T(8,128)(2,1)} copy(bf16[128,4096]{1,0:T(8,128)(2,1)} %get-tuple-element.4) | data formatting | bytes 2097152
  87.2 0.0 copy-done
  87.2 0.6 copy.14
Async XLA Ops:
  84.9 2.3 %copy-start = (f32[12,1024]{1,0:T(8,128)S(1)}, f32[12,1024]{1,0:T(8,128)}, u32[]{:S(2)}) copy-start(f32[12,1024]{1,0:T(8,128)} %get-tuple-element.5) | copy-start | bytes 147460

commit v6 on v5

--- a/solution.py
+++ b/solution.py
@@ -287,7 +287,7 @@
 
     def copy2(kind, s, k):
         return remote(
-            chosen.at[kind, s, k], win.at[kind, s, piece_here], send2, recv2.at[s], (dp, reader(k))
+            chosen.at[kind, s, k], win.at[kind, s, piece_here], send2, recv2.at[s, lax.rem(k, N_X)], (dp, reader(k))
         )
 
     for kind in range(2):
@@ -295,7 +295,8 @@
         for s in range(2):
 
             def serve(k, kind=kind, s=s):
-                k = 1 + lax.rem(k + 6, N_PIECE - 1)
+                n = k - N_X
+                k = jnp.where(n < 0, k * N_X, lax.rem(n, N_ROW) * N_X + N_X - 1 - n // N_ROW)
                 choose(kind, s, k)
                 copy2(kind, s, k).start()
 
@@ -334,7 +335,6 @@
         return jnp.concatenate([ref[rows, lanes((j * G + g) * HD, HD)] for g in range(G)], axis=0)
 
     for s in range(2):
-        settle(win.at[:, s, pl.ds(0, N_PIECE - 1)], recv2.at[s])
 
         def attend(n, s=s):
             j = lax.rem(x + n, KVH)
@@ -365,7 +365,13 @@
             dk = jnp.dot(kept_ds[s, j], stacked(qrot, s, j), preferred_element_type=F32)
             hand_over(0, s, n, dk * SCALE)
 
-        loop(0, KVH, attend)
+        def attend_next(n, s=s):
+            settle(win.at[:, s, pl.ds(0, N_ROW)], recv2.at[s, N_X - n])
+            attend(n)
+
+        settle(win.at[:, s, pl.ds(0, N_ROW - 1)], recv2.at[s, 0])
+        attend(0)
+        loop(1, KVH, attend_next)
         loop(0, KVH, key_part)
         for kind in range(2):
             landed[kind][pl.ds(REACH * me + BACK * s, BACK)] = part[kind, s, piece_here]
@@ -386,7 +392,7 @@
 
     def copy4(kind, src, owner, peer):
         return remote(
-            total.at[kind, src], back.at[kind, owner], send4, recv4.at[kind], (dp, peer)
+            total.at[kind, src], back.at[kind, owner], send4.at[kind], recv4.at[kind], (dp, peer)
         )
 
     def sum_up(kind, device):
@@ -399,6 +405,8 @@
 
     for kind in (1, 0):
         settle(landed[kind].at[pl.ds(0, REACH * (N_PIECE - 1))], recv3.at[kind])
+        if kind == 0:
+            settle(total.at[1, pl.ds(0, N_CTX - 1)], send4.at[1])
 
         def give_back(k, kind=kind):
             sum_up(kind, far_peer(k))
@@ -490,7 +498,7 @@
     settle(xt.at[:, pl.ds(0, (N_DP - 1) * ROWS)], send5)
     settle(chosen.at[:, :, pl.ds(0, N_PIECE - 1)], send2)
     settle(part.at[:, :, pl.ds(0, N_PIECE - 1)], send3)
-    settle(total.at[:, pl.ds(0, N_CTX - 1)], send4)
+    settle(total.at[0, pl.ds(0, N_CTX - 1)], send4.at[0])
     settle(grads.at[:, 0, pl.ds(0, LINE - 1)], send6)
     settle(grads.at[:, 0], send7)
     settle(wsend.at[:, pl.ds(0, LINE - 1)], send8)
@@ -552,9 +560,9 @@
             vmem((CHUNKS, N_Z, PIECE, W_COL), BF16),
             dma((11,)),
             dma((2,)), dma((2,)),
+            dma, dma((2, N_X)),
             dma, dma((2,)),
-            dma, dma((2,)),
-            dma, dma((2,)),
+            dma((2,)), dma((2,)),
             dma, dma,
             dma, dma((CHUNKS,)),
             dma, dma((CHUNKS,)),

time: 87.9 us -> 86.6 us (0.985)
  Pallas kernels: 84.2 us -> 82.9 us
    pallas_call x1, Pallas kernels: 84.2 us -> 82.9 us  [per_device(): pl.pallas_call(kernel, out_shape=[jax.ShapeDtypeStruct((ROWS, wide), BF16...]
where the time goes in v6:
time: 86.6 us; the launch traced here: 86.5 us
  Pallas kernels  82.9 us (96%)
  local copies, waits for them, and re-layouts  2.95 us (3%)
    pallas_call x1, Pallas kernels, per_device(): pl.pallas_call(kernel, out_shape=[jax.ShapeDtypeStruct((ROWS, wide), BF16...  82.9 us
    unnamed x4, local copies, waits for them, and re-layouts  2.95 us

profile of v6, /device:TPU:1, one launch (start us, length us, event | category | flops | bytes accessed | tf_op | source)
XLA Modules:
  0.0 86.5 jit_solution(4124603242830820614)
XLA Ops:
  0.6 82.9 %packed_backward.1 = (bf16[128,4096]{1,0:T(8,128)(2,1)}, f32[12,1024]{1,0:T(8,128)}) custom-call(s32[1,64]{1,0:T(1,128)} %span_h.1, s32[1,32]{1,0:T(1,128)} %len_h.1, f32[1,128]{1,0:T(1,128)} %constant.4.clone.freq_h, bf16[384,384]{1,0:T(8,128)(2,1)} %constant.5.clone.perm_h, bf16[128,4096]{1,0:T(8,128)(2,1)} %q_h.1, bf16[128,512]{1,0:T(8,128)(2,1)} %k_h.1, ...), custom_call_target="tpu_custom_call" | custom-call | tf_op jit(solution)/shard_map/packed_backward/pallas_call | solution.py:514
  83.6 0.0 copy-start
  83.6 2.3 %copy.13 = bf16[128,4096]{1,0:T(8,128)(2,1)} copy(bf16[128,4096]{1,0:T(8,128)(2,1)} %get-tuple-element.4) | data formatting | bytes 2097152
  85.9 0.0 copy-done
  85.9 0.6 copy.14
Async XLA Ops:
  83.6 2.3 %copy-start = (f32[12,1024]{1,0:T(8,128)S(1)}, f32[12,1024]{1,0:T(8,128)}, u32[]{:S(2)}) copy-start(f32[12,1024]{1,0:T(8,128)} %get-tuple-element.5) | copy-start | bytes 147460

commit v7 on v6

--- a/solution.py
+++ b/solution.py
@@ -37,7 +37,7 @@
 W_DP = DW // N_DP
 W_DEV = W_DP // N_CTX
 W_X = W_DP // N_X
-CHUNKS = 4
+CHUNKS = 8
 HEADS = 2 * KVH // CHUNKS
 W_COL = 2 * KVC // CHUNKS
 N_Y = N_DP // 2
@@ -290,19 +290,23 @@
             chosen.at[kind, s, k], win.at[kind, s, piece_here], send2, recv2.at[s, lax.rem(k, N_X)], (dp, reader(k))
         )
 
-    for kind in range(2):
-        settle(held[kind].at[pl.ds(0, 2 * (N_CTX - 1))], recv1.at[kind])
-        for s in range(2):
-
-            def serve(k, kind=kind, s=s):
-                n = k - N_X
-                k = jnp.where(n < 0, k * N_X, lax.rem(n, N_ROW) * N_X + N_X - 1 - n // N_ROW)
-                choose(kind, s, k)
-                copy2(kind, s, k).start()
-
-            loop(1, N_PIECE, serve)
-            choose(kind, s, 0)
-            win[kind, s, piece_here] = chosen[kind, s, 0]
+    def hand_out(kind, s):
+        def serve(k):
+            n = k - N_X
+            k = jnp.where(n < 0, k * N_X, lax.rem(n, N_ROW) * N_X + N_X - 1 - n // N_ROW)
+            choose(kind, s, k)
+            copy2(kind, s, k).start()
+
+        loop(1, N_PIECE, serve)
+        choose(kind, s, 0)
+        win[kind, s, piece_here] = chosen[kind, s, 0]
+
+    settle(held[0].at[pl.ds(0, 2 * (N_CTX - 1))], recv1.at[0])
+    hand_out(0, 0)
+    settle(held[1].at[pl.ds(0, 2 * (N_CTX - 1))], recv1.at[1])
+    hand_out(1, 0)
+    hand_out(0, 1)
+    hand_out(1, 1)
     fetches[8].wait()
 
     def copy3(kind, s, k):

time: 86.6 us -> 85.6 us (0.988)
  Pallas kernels: 82.9 us -> 81.9 us
    pallas_call x1, Pallas kernels: 82.9 us -> 81.9 us  [per_device(): pl.pallas_call(kernel, out_shape=[jax.ShapeDtypeStruct((ROWS, wide), BF16...]
where the time goes in v7:
time: 85.6 us; the launch traced here: 85.5 us
  Pallas kernels  81.9 us (96%)
  local copies, waits for them, and re-layouts  2.95 us (3%)
    pallas_call x1, Pallas kernels, per_device(): pl.pallas_call(kernel, out_shape=[jax.ShapeDtypeStruct((ROWS, wide), BF16...  81.9 us
    unnamed x4, local copies, waits for them, and re-layouts  2.95 us

profile of v7, /device:TPU:1, one launch (start us, length us, event | category | flops | bytes accessed | tf_op | source)
XLA Modules:
  0.0 85.5 jit_solution(11356060567543936808)
XLA Ops:
  0.6 81.9 %packed_backward.1 = (bf16[128,4096]{1,0:T(8,128)(2,1)}, f32[12,1024]{1,0:T(8,128)}) custom-call(s32[1,64]{1,0:T(1,128)} %span_h.1, s32[1,32]{1,0:T(1,128)} %len_h.1, f32[1,128]{1,0:T(1,128)} %constant.4.clone.freq_h, bf16[384,384]{1,0:T(8,128)(2,1)} %constant.5.clone.perm_h, bf16[128,4096]{1,0:T(8,128)(2,1)} %q_h.1, bf16[128,512]{1,0:T(8,128)(2,1)} %k_h.1, ...), custom_call_target="tpu_custom_call" | custom-call | tf_op jit(solution)/shard_map/packed_backward/pallas_call | solution.py:518
  82.5 0.0 copy-start
  82.5 2.3 %copy.13 = bf16[128,4096]{1,0:T(8,128)(2,1)} copy(bf16[128,4096]{1,0:T(8,128)(2,1)} %get-tuple-element.4) | data formatting | bytes 2097152
  84.8 0.0 copy-done
  84.8 0.6 copy.14
Async XLA Ops:
  82.5 2.3 %copy-start = (f32[12,1024]{1,0:T(8,128)S(1)}, f32[12,1024]{1,0:T(8,128)}, u32[]{:S(2)}) copy-start(f32[12,1024]{1,0:T(8,128)} %get-tuple-element.5) | copy-start | bytes 147460

commit v8 on v7

--- a/solution.py
+++ b/solution.py
@@ -134,6 +134,13 @@
         step = n // 2 + 1
         return ctx_peer(jnp.where(lax.rem(n, 2) == 0, step, N_CTX - step))
 
+    far_step = lambda k: 1 + lax.rem(k, LINE - 1)
+
+    def far_z(k):
+        n = N_Z - 1 - k
+        step = n // 2 + 1
+        return jnp.where(lax.rem(n, 2) == 0, step, N_Z - step)
+
     dp_peer = lambda k: lax.rem(dp + k, N_DP)
     y_peer = lambda k: lax.rem(dp + 2 * k, N_DP)
     x_peer = lambda k: lax.rem(x + k, N_X)
@@ -441,7 +448,7 @@
                         at = slice(BACK * SPAN + r * PIECE, BACK * SPAN + (r + 1) * PIECE)
                         g = g * cos[s, at] - swap_halves(g) * sin[s, at]
                     grads[c, core, y, rows, n * HD : (n + 1) * HD] = g.astype(BF16)
-        loop(1, LINE, lambda k: copy6(c, k).start())
+        loop(1, LINE, lambda k: copy6(c, far_step(k)).start())
 
     def forward(c):
         settle(grads.at[c, 0, pl.ds(0, LINE - 1)], recv6.at[c])
@@ -458,7 +465,7 @@
         settle(grads.at[c, 0], recv7.at[c])
         w = jnp.dot(xt[...], grads[c].reshape(N_DP * ROWS, W_COL), preferred_element_type=F32)
         wsend[c] = w.astype(BF16).reshape(LINE, W_X, W_COL)
-        loop(1, LINE, lambda k: copy8(c, k).start())
+        loop(1, LINE, lambda k: copy8(c, far_step(k)).start())
         wland[c, x] = wsend[c, x]
 
     def sum_line(c):
@@ -470,7 +477,7 @@
         for n in range(N_Z):
             block = jnp.concatenate([acc[n * W_DEV : (n + 1) * W_DEV], pad], axis=0)
             zsend[c, n] = block.astype(BF16)
-        loop(1, N_Z, lambda k: copy9(c, z_peer(k)).start())
+        loop(1, N_Z, lambda k: copy9(c, z_peer(far_z(k))).start())
         zland[c, z] = zsend[c, z]
 
     def sum_z(c):

time: 85.6 us -> 85.2 us (level)
  no operation moved by 1% of the time
where the time goes in v8:
time: 85.2 us; the launch traced here: 85.1 us
  Pallas kernels  81.5 us (96%)
  local copies, waits for them, and re-layouts  2.95 us (3%)
    pallas_call x1, Pallas kernels, per_device(): pl.pallas_call(kernel, out_shape=[jax.ShapeDtypeStruct((ROWS, wide), BF16...  81.5 us
    unnamed x4, local copies, waits for them, and re-layouts  2.95 us

profile of v8, /device:TPU:1, one launch (start us, length us, event | category | flops | bytes accessed | tf_op | source)
XLA Modules:
  0.0 85.1 jit_solution(12375646420144334735)
XLA Ops:
  0.6 81.5 %packed_backward.1 = (bf16[128,4096]{1,0:T(8,128)(2,1)}, f32[12,1024]{1,0:T(8,128)}) custom-call(s32[1,64]{1,0:T(1,128)} %span_h.1, s32[1,32]{1,0:T(1,128)} %len_h.1, f32[1,128]{1,0:T(1,128)} %constant.4.clone.freq_h, bf16[384,384]{1,0:T(8,128)(2,1)} %constant.5.clone.perm_h, bf16[128,4096]{1,0:T(8,128)(2,1)} %q_h.1, bf16[128,512]{1,0:T(8,128)(2,1)} %k_h.1, ...), custom_call_target="tpu_custom_call" | custom-call | tf_op jit(solution)/shard_map/packed_backward/pallas_call | solution.py:525
  82.1 0.0 copy-start
  82.1 2.3 %copy.13 = bf16[128,4096]{1,0:T(8,128)(2,1)} copy(bf16[128,4096]{1,0:T(8,128)(2,1)} %get-tuple-element.4) | data formatting | bytes 2097152
  84.4 0.0 copy-done
  84.4 0.6 copy.14
Async XLA Ops:
  82.1 2.3 %copy-start = (f32[12,1024]{1,0:T(8,128)S(1)}, f32[12,1024]{1,0:T(8,128)}, u32[]{:S(2)}) copy-start(f32[12,1024]{1,0:T(8,128)} %get-tuple-element.5) | copy-start | bytes 147460
